TPU v7x, 32 devices: a whole 2x2x4 slice. The times are simulated.
32 devices in a mesh: seq: 4 (over x, core), batch: 8 (over z, y).
Axes of the slice: x: 2, y: 2, z: 4, core: 2. Of those that a mesh axis runs over, the one named last changes fastest.
Arguments:
- hidden: bfloat16 [24, 1024, 768], P('batch', 'seq'), may hold values from -6 to 6
- cond: float32 [24, 128], P('batch'), may hold values from -6 to 6
- lengths: int32 [24, 8], P('batch'), may hold values from 1 to 1017, as said below
- ln1_gain: float32 [768], replicated, may hold values from 0.25 to 1.75
- w_qkv: bfloat16 [768, 2304], replicated, may hold values from -0.21875 to 0.21875
- w_out: bfloat16 [768, 768], replicated, may hold values from -1.75 to 1.75
- ln2_gain: float32 [768], replicated, may hold values from 0.25 to 1.75
- w_fc1: bfloat16 [768, 3072], replicated, may hold values from -0.21875 to 0.21875
- b_fc1: float32 [3072], replicated, may hold values from -3 to 3
- w_fc2: bfloat16 [3072, 768], replicated, may hold values from -0.109375 to 0.109375
- b_fc2: float32 [768], replicated, may hold values from -2 to 2
- w_ada: bfloat16 [128, 4608], replicated, may hold values from -0.25 to 0.25
- b_ada: float32 [4608], replicated, may hold values from -2 to 2
- cotangent: bfloat16 [24, 1024, 768], P('batch', 'seq'), may hold values from -6 to 6
Outputs:
- output: bfloat16 [24, 1024, 768], P('batch', 'seq')
- hidden_grad: bfloat16 [24, 1024, 768], P('batch', 'seq')
- cond_grad: float32 [24, 128], P('batch')
- ln1_gain_grad: float32 [768], replicated
- w_qkv_grad: float32 [768, 2304], replicated
- w_out_grad: float32 [768, 768], replicated
- ln2_gain_grad: float32 [768], replicated
- w_fc1_grad: float32 [768, 3072], replicated
- b_fc1_grad: float32 [3072], replicated
- w_fc2_grad: float32 [3072, 768], replicated
- b_fc2_grad: float32 [768], replicated
- w_ada_grad: float32 [128, 4608], replicated
- b_ada_grad: float32 [4608], replicated
Inputs may be any that keep to these rules, and one draw needn't show every extreme that they name: Each row's 8 lengths sum to 1024; in every row one document starts within the first 256 slots and ends within the last 256 slots.
All inputs are finite; a program needn't handle non-finite values.
Results may differ from a plain program's by a relative error of at most 0.015.
The roundings to bfloat16 on the way count: a program that leaves them out, or rounds other values in their place, can miss the bound.
Values may be sent and summed in bfloat16 or wider, within the bound.
No kernel may reach another device: no remote copies, remote signals or barrier semaphores. Data moves between devices by JAX's collectives and lax.ppermute only.
A program may use at most 320 MiB of HBM per device.

v0:
```python
import jax
import jax.numpy as jnp
from jax import lax
from jax.sharding import PartitionSpec as P

HEADS = 12
HEAD = 64


highest = lax.Precision.HIGHEST


def layer_norm(values, gain):
    center = values - jnp.mean(values, axis=-1, keepdims=True)
    spread = jnp.mean(center * center, axis=-1, keepdims=True)
    return center * lax.rsqrt(spread + 1e-05) * gain


def modulate(values, gain, shift, scale):
    return layer_norm(values, gain) * (1.0 + scale) + shift


def gelu_tanh(values):
    return jax.nn.gelu(values, approximate=True)


def rotate(values, places):
    shape_in = values.shape
    heads_view = values.reshape(shape_in[0], shape_in[1], HEADS, HEAD)
    half_dim = HEAD // 2
    inverse_freq = 10000.0 ** (-jnp.arange(half_dim, dtype=jnp.float32) * 2.0 / HEAD)
    angles = places.astype(jnp.float32)[:, :, None] * inverse_freq
    cosine = jnp.cos(angles)[:, :, None, :]
    sine = jnp.sin(angles)[:, :, None, :]
    front = heads_view[..., :half_dim]
    behind = heads_view[..., half_dim:]
    turned = jnp.concatenate(
        [front * cosine - behind * sine, behind * cosine + front * sine], axis=-1
    )
    return turned.reshape(shape_in)


def doc_layout(lengths, slots):
    bounds = jnp.cumsum(lengths, axis=1)
    passed = (slots[None, :, None] >= bounds[:, None, :]).astype(jnp.int32)
    segment = jnp.sum(passed, axis=2)
    doc_start = jnp.sum(passed * lengths[:, None, :], axis=2)
    return (segment, slots[None, :] - doc_start)


def outer(left, right):
    return lax.dot_general(
        left, right, (((0,), (0,)), ((), ())), preferred_element_type=jnp.float32
    )


def against(values, weight):
    return lax.dot_general(
        values, weight, (((1,), (1,)), ((), ())), preferred_element_type=jnp.float32
    )


def scores_of(query, keys, query_seg, key_seg):
    query_heads = query.reshape(query.shape[0], HEADS, HEAD)
    key_heads = keys.reshape(keys.shape[0], HEADS, HEAD)
    scores = (
        jnp.einsum("chd,khd->hck", query_heads, key_heads, preferred_element_type=jnp.float32)
        * 0.125
    )
    return jnp.where(query_seg[None, :, None] == key_seg[None, None, :], scores, -1e30)


def attend(operands):
    query, keys, values, query_seg, key_seg = operands
    scores = scores_of(query, keys, query_seg, key_seg)
    peak = jnp.max(scores, axis=-1, keepdims=True)
    expo = jnp.exp(scores - peak)
    total_sum = jnp.sum(expo, axis=-1, keepdims=True)
    probs = (expo / total_sum).astype(jnp.bfloat16)
    value_heads = values.reshape(values.shape[0], HEADS, HEAD)
    mixed = jnp.einsum("hck,khd->chd", probs, value_heads, preferred_element_type=jnp.float32)
    return (mixed.reshape(query.shape[0], HEADS * HEAD), peak[..., 0] + jnp.log(total_sum[..., 0]))


def attend_back(operands):
    query, keys, values, mixed_grad, logsum, query_seg, key_seg = operands
    scores = scores_of(query, keys, query_seg, key_seg)
    probs = jnp.exp(scores - logsum[:, :, None])
    probs_low = probs.astype(jnp.bfloat16)
    grad_heads = mixed_grad.reshape(query.shape[0], HEADS, HEAD)
    query_heads = query.reshape(query.shape[0], HEADS, HEAD)
    key_heads = keys.reshape(keys.shape[0], HEADS, HEAD)
    value_heads = values.reshape(values.shape[0], HEADS, HEAD)
    value_grad = jnp.einsum(
        "hck,chd->khd", probs_low, grad_heads, preferred_element_type=jnp.float32
    )
    prob_grad = jnp.einsum(
        "chd,khd->hck", grad_heads, value_heads, preferred_element_type=jnp.float32
    )
    score_grad = (probs * (prob_grad - jnp.sum(probs * prob_grad, axis=-1, keepdims=True))).astype(
        jnp.bfloat16
    )
    query_grad = 0.125 * jnp.einsum(
        "hck,khd->chd", score_grad, key_heads, preferred_element_type=jnp.float32
    )
    key_grad = 0.125 * jnp.einsum(
        "hck,chd->khd", score_grad, query_heads, preferred_element_type=jnp.float32
    )
    return (
        query_grad.reshape(query.shape[0], -1),
        key_grad.reshape(keys.shape[0], -1),
        value_grad.reshape(keys.shape[0], -1),
    )


def shards(
    hidden,
    cond,
    lengths,
    ln1_gain,
    w_qkv,
    w_out,
    ln2_gain,
    w_fc1,
    b_fc1,
    w_fc2,
    b_fc2,
    w_ada,
    b_ada,
    cotangent,
):
    row_count, span_len, features = hidden.shape
    full_len = span_len * lax.axis_size("seq")
    offset = lax.axis_index("seq") * span_len
    query_seg, query_place = doc_layout(lengths, offset + jnp.arange(span_len, dtype=jnp.int32))
    key_seg, key_place = doc_layout(lengths, jnp.arange(full_len, dtype=jnp.int32))
    inputs = hidden.astype(jnp.float32)
    ada_full = w_ada.astype(jnp.float32)
    modulation = (
        jnp.dot(cond, ada_full, precision=highest, preferred_element_type=jnp.float32) + b_ada
    )
    shift_one, scale_one, gate_one, shift_two, scale_two, gate_two = [
        column[:, None, :] for column in jnp.split(modulation, 6, axis=1)
    ]
    normed, norm_one_back = jax.vjp(modulate, inputs, ln1_gain, shift_one, scale_one)
    normed_low = normed.astype(jnp.bfloat16)
    merged = jnp.dot(normed_low.reshape(-1, features), w_qkv, preferred_element_type=jnp.float32)
    merged = merged.reshape(row_count, span_len, 3 * features)

    def rotate_pair(query_in, key_in):
        return (rotate(query_in, query_place), rotate(key_in, query_place))

    (query_rot, key_rot), rotate_back = jax.vjp(
        rotate_pair, merged[..., :features], merged[..., features : 2 * features]
    )
    query_low = query_rot.astype(jnp.bfloat16)
    key_low = key_rot.astype(jnp.bfloat16)
    value_low = merged[..., 2 * features :].astype(jnp.bfloat16)
    keys_all, values_all = (
        lax.all_gather(key_low, "seq", axis=1, tiled=True),
        lax.all_gather(value_low, "seq", axis=1, tiled=True),
    )
    mixed, logsum = lax.map(attend, (query_low, keys_all, values_all, query_seg, key_seg))
    mixed_low = mixed.astype(jnp.bfloat16)
    attended = jnp.dot(
        mixed_low.reshape(-1, features), w_out, preferred_element_type=jnp.float32
    ).reshape(row_count, span_len, features)
    resid = inputs + gate_one * attended
    second, norm_two_back = jax.vjp(modulate, resid, ln2_gain, shift_two, scale_two)
    second_low = second.astype(jnp.bfloat16).reshape(-1, features)
    hidden_pre = jnp.dot(second_low, w_fc1, preferred_element_type=jnp.float32) + b_fc1
    active, gelu_back = jax.vjp(gelu_tanh, hidden_pre)
    active_low = active.astype(jnp.bfloat16)
    branch = (jnp.dot(active_low, w_fc2, preferred_element_type=jnp.float32) + b_fc2).reshape(
        row_count, span_len, features
    )
    output = (resid + gate_two * branch).astype(jnp.bfloat16)
    upstream = cotangent.astype(jnp.float32)
    gate_two_grad = jnp.sum(upstream * branch, axis=1)
    branch_grad = gate_two * upstream
    branch_low = branch_grad.astype(jnp.bfloat16).reshape(-1, features)
    fc2_grad = outer(active_low, branch_low)
    fc2_bias_grad = jnp.sum(branch_grad, axis=(0, 1))
    active_grad = against(branch_low, w_fc2)
    pre_grad = gelu_back(active_grad)[0]
    pre_low = pre_grad.astype(jnp.bfloat16)
    fc1_bias_grad = jnp.sum(pre_grad, axis=0)
    fc1_grad = outer(second_low, pre_low)
    second_grad = against(pre_low, w_fc1).reshape(row_count, span_len, features)
    resid_part, gain_two_grad, shift_two_grad, scale_two_grad = norm_two_back(second_grad)
    resid_grad = upstream + resid_part
    gate_one_grad = jnp.sum(resid_grad * attended, axis=1)
    attended_low = (gate_one * resid_grad).astype(jnp.bfloat16).reshape(-1, features)
    out_grad = outer(mixed_low.reshape(-1, features), attended_low)
    mixed_grad = (
        against(attended_low, w_out).astype(jnp.bfloat16).reshape(row_count, span_len, features)
    )
    keys_back, values_back = (
        lax.all_gather(key_low, "seq", axis=1, tiled=True),
        lax.all_gather(value_low, "seq", axis=1, tiled=True),
    )
    query_grad, key_grad_all, value_grad_all = lax.map(
        attend_back, (query_low, keys_back, values_back, mixed_grad, logsum, query_seg, key_seg)
    )
    key_grad, value_grad = (
        lax.psum_scatter(
            key_grad_all.astype(jnp.bfloat16), "seq", scatter_dimension=1, tiled=True
        ).astype(jnp.float32),
        lax.psum_scatter(
            value_grad_all.astype(jnp.bfloat16), "seq", scatter_dimension=1, tiled=True
        ).astype(jnp.float32),
    )
    query_pre, key_pre = rotate_back((query_grad, key_grad))
    merged_grad = (
        jnp.concatenate([query_pre, key_pre, value_grad], axis=-1)
        .astype(jnp.bfloat16)
        .reshape(-1, 3 * features)
    )
    qkv_grad = outer(normed_low.reshape(-1, features), merged_grad)
    normed_grad = against(merged_grad, w_qkv).reshape(row_count, span_len, features)
    input_part, gain_one_grad, shift_one_grad, scale_one_grad = norm_one_back(normed_grad)
    hidden_grad = (resid_grad + input_part).astype(jnp.bfloat16)
    mod_local = jnp.concatenate(
        [
            shift_one_grad[:, 0, :],
            scale_one_grad[:, 0, :],
            gate_one_grad,
            shift_two_grad[:, 0, :],
            scale_two_grad[:, 0, :],
            gate_two_grad,
        ],
        axis=1,
    )
    ada_grad = jnp.dot(cond.T, mod_local, precision=highest, preferred_element_type=jnp.float32)
    ada_bias_grad = jnp.sum(mod_local, axis=0)
    mod_total = lax.psum(mod_local.astype(jnp.bfloat16), "seq").astype(jnp.float32)
    cond_grad = jnp.dot(
        mod_total, ada_full.T, precision=highest, preferred_element_type=jnp.float32
    )
    grad_list = [
        gain_one_grad,
        qkv_grad,
        out_grad,
        gain_two_grad,
        fc1_grad,
        fc1_bias_grad,
        fc2_grad,
        fc2_bias_grad,
        ada_grad,
        ada_bias_grad,
    ]
    flat = jnp.concatenate([tensor.reshape(-1) for tensor in grad_list])
    shard_count = lax.axis_size("seq") * lax.axis_size("batch")
    unit_len = 128 * shard_count
    padded_len = -(-flat.shape[0] // unit_len) * unit_len
    flat = jnp.pad(flat, (0, padded_len - flat.shape[0]))
    share_len = padded_len // shard_count
    spread_flat = flat.reshape(share_len, shard_count).T.reshape(-1)
    joint_share = lax.psum_scatter(spread_flat, ("seq", "batch"), scatter_dimension=0, tiled=True)
    gathered = lax.all_gather(
        joint_share.astype(jnp.bfloat16), ("seq", "batch"), axis=0, tiled=True
    ).astype(joint_share.dtype)
    summed = gathered.reshape(shard_count, share_len).T.reshape(-1)
    results = []
    cursor = 0
    for tensor in grad_list:
        element_count = tensor.size
        results.append(summed[cursor : cursor + element_count].reshape(tensor.shape))
        cursor = cursor + element_count
    return (
        output,
        hidden_grad,
        cond_grad,
        results[0],
        results[1],
        results[2],
        results[3],
        results[4],
        results[5],
        results[6],
        results[7],
        results[8],
        results[9],
    )


def solution(mesh):
    return jax.shard_map(
        shards,
        mesh=mesh,
        in_specs=(
            P("batch", "seq", None),
            P("batch", None),
            P("batch", None),
            P(),
            P(),
            P(),
            P(),
            P(),
            P(),
            P(),
            P(),
            P(),
            P(),
            P("batch", "seq", None),
        ),
        out_specs=(
            P("batch", "seq", None),
            P("batch", "seq", None),
            P("batch", None),
            P(),
            P(),
            P(),
            P(),
            P(),
            P(),
            P(),
            P(),
            P(),
            P(),
        ),
        check_vma=False,
    )
```

profile of v0, /device:TPU:0, one launch (start us, length us, event | category | flops | bytes accessed | tf_op | source)
XLA Modules:
  0.0 1851.0 jit_solution(151635771860190535)
XLA Ops:
  44.7 15.5 all-gather.5.cloned.1.call-done
  66.8 33.6 %all-gather.7.cloned.1.call-done = bf16[3,1024,768]{1,2,0:T(8,128)(2,1)} async-done(((bf16[3,256,768]{1,2,0:T(8,128)(2,1)}), bf16[3,1024,768]{1,2,0:T(8,128)(2,1)}) %all-gather.7.cloned.1.call-update) | async-done | bytes 4718608 | tf_op jit(solution)/shard_map/all_gather | solution.py:160
  100.4 46.4 %while.28 = (s32[]{:T(128)}, bf16[3,256,768]{1,2,0:T(8,128)(2,1)}, f32[3,12,256]{2,1,0:T(8,128)}, bf16[3,1024,768]{1,2,0:T(8,128)(2,1)}, s32[3,256]{1,0:T(4,128)...) while((s32[]{:T(128)}, bf16[3,256,768]{1,2,0:T(8,128)(2,1)}, ...), condition=%wide.region_9.10_spmd.clone, body=%wide.region_6.9_spmd.sunk.clone | while | flops 843314176 | bytes 50711668 | solution.py:163
  194.4 159.6 %while.29 = (s32[]{:T(128)}, f32[3,256,768]{1,2,0:T(8,128)}, bf16[3,1024,768]{1,2,0:T(8,128)(2,1)}, bf16[3,1024,768]{2,1,0:T(8,128)(2,1)}, bf16[3,1024,768]{1,2,...) while((s32[]{:T(128)}, f32[3,256,768]{1,2,0:T(8,128)}, ...), condition=%wide.region_16.17_spmd.clone, body=%wide.region_14.16_spmd.sunk.clone | while | flops 2062480384 | bytes 181603792 | solution.py:202
  375.4 13.2 fusion.54
  412.1 40.3 %reduce-scatter.5.cloned.1.call-done = bf16[3,256,768]{2,1,0:T(8,128)(2,1)} async-done(((bf16[3,1024,768]{2,1,0:T(8,128)(2,1)}), bf16[3,256,768]{2,1,0:T(8,128)(2,1)}) %reduce-scatter.5.cloned.1.call-update) | async-done | bytes 1179664 | tf_op jit(solution)/shard_map/reduce_scatter | solution.py:209
  486.0 60.7 %dynamic-update-slice.1 = f32[7677696]{0:T(1024)} dynamic-update-slice(f32[7677696]{0:T(1024)} %constant_dynamic-update-slice_fusion.10, f32[1769472]{0:T(1024)} %reshape.397, s32[]{} %constant.123) | dynamic-update-slice | bytes 14155780
  546.7 20.1 %dynamic-update-slice.2 = f32[7677696]{0:T(1024)} dynamic-update-slice(f32[7677696]{0:T(1024)} %dynamic-update-slice.1, f32[589824]{0:T(1024)S(1)} %copy-done.17, s32[]{} %constant.124) | dynamic-update-slice | bytes 4718596
  568.1 80.4 %dynamic-update-slice.4 = f32[7677696]{0:T(1024)} dynamic-update-slice(f32[7677696]{0:T(1024)} %constant_dynamic-update-slice_fusion.14, f32[2359296]{0:T(1024)} %bitcast.210, s32[]{} %constant.126) | dynamic-update-slice | bytes 18874372
  649.9 80.8 %dynamic-update-slice.6 = f32[7677696]{0:T(1024)} dynamic-update-slice(f32[7677696]{0:T(1024)} %constant_dynamic-update-slice_fusion.13, f32[2359296]{0:T(1024)} %reshape.400, s32[]{} %constant.128) | dynamic-update-slice | bytes 18874372
  731.9 20.1 %dynamic-update-slice.8 = f32[7677696]{0:T(1024)} dynamic-update-slice(f32[7677696]{0:T(1024)} %constant_dynamic-update-slice_fusion.12, f32[589824]{0:T(1024)S(1)} %copy-done.18, s32[]{} %constant.130) | dynamic-update-slice | bytes 4718596
  753.4 22.0 %pad.20 = f32[7680000]{0:T(1024)} pad(f32[7677696]{0:T(1024)} %constant_dynamic-update-slice_fusion.11, f32[]{:T(128)} %constant.91.clone.1), padding=0_2304 | pad | bytes 61430788 | tf_op jit(solution)/shard_map/jit(_pad)/pad | solution.py:256
  775.4 72.3 %reshape.402 = f32[240000,32]{1,0:T(8,128)} reshape(f32[7680000]{0:T(1024)} %pad.20) | data formatting | bytes 61440000 | tf_op jit(solution)/shard_map/reshape | solution.py:258
  847.7 72.6 %copy.113 = f32[32,240000]{1,0:T(8,128)} copy(f32[32,240000]{0,1:T(8,128)} %bitcast.41) | data formatting | bytes 61440000 | tf_op jit(solution)/shard_map/transpose | solution.py:258
  920.3 26.9 %reshape.403 = f32[7680000]{0:T(1024)} reshape(f32[32,240000]{1,0:T(8,128)} %copy.113) | data formatting | bytes 61440000 | tf_op jit(solution)/shard_map/reshape | solution.py:258
  947.2 493.8 %all-reduce.7 = bf16[7680000]{0:T(1024)(128)(2,1)} all-reduce(f32[7680000]{0:T(1024)} %reshape.403), channel_id=4, replica_groups=mesh['seq'=4,'batch'=8] {'seq','batch'}, use_global_device_ids=true, to_apply=%region_33.34.clone | all-reduce | flops 7680000 | bytes 46080000
  1467.7 160.0 %all-gather.9.cloned.1.call-done = bf16[32,1,240000]{2,1,0:T(2,128)(2,1)} async-done(((bf16[1,1,240000]{2,1,0:T(2,128)(2,1)}), bf16[32,1,240000]{2,1,0:T(2,128)(2,1)}) %all-gather.9.cloned.1.call-update) | async-done | bytes 15360016 | tf_op jit(solution)/shard_map/all_gather | solution.py:260
  1627.7 13.8 copy.156
  1680.6 16.2 copy.115
  1696.7 19.3 %reshape.405 = f32[768,2304]{1,0:T(8,128)} reshape(f32[55296,32]{1,0:T(8,128)} %copy.115) | data formatting | bytes 14155776 | tf_op jit(solution)/shard_map/reshape | solution.py:268
  1730.9 21.0 %copy.118 = f32[73728,32]{1,0:T(8,128)} copy(f32[73728,32]{0,1:T(8,128)} %get-tuple-element.286) | data formatting | bytes 18874368 | tf_op jit(solution)/shard_map/slice | solution.py:268
  1751.9 27.7 %reshape.407 = f32[768,3072]{1,0:T(8,128)} reshape(f32[73728,32]{1,0:T(8,128)} %copy.118) | data formatting | bytes 18874368 | tf_op jit(solution)/shard_map/reshape | solution.py:268
  1780.4 21.0 %copy.120 = f32[73728,32]{1,0:T(8,128)} copy(f32[73728,32]{0,1:T(8,128)} %get-tuple-element.285) | data formatting | bytes 18874368 | tf_op jit(solution)/shard_map/slice | solution.py:268
  1801.4 25.8 %reshape.408 = f32[3072,768]{1,0:T(8,128)} reshape(f32[73728,32]{1,0:T(8,128)} %copy.120) | data formatting | bytes 18874368 | tf_op jit(solution)/shard_map/reshape | solution.py:268
  (402 shorter events, 478.5 us)
Async XLA Ops:
  7.2 53.0 %all-gather.5.cloned.1.call-start = ((), (), s32[]{:S(2)}) async-start(), calls=%async_computation.2 | async-start | bytes 5898240 | tf_op jit(solution)/shard_map/all_gather | solution.py:161
  19.9 80.5 %all-gather.7.cloned.1.call-start = ((), (), s32[]{:S(2)}) async-start(), calls=%async_computation.3 | async-start | bytes 5898240 | tf_op jit(solution)/shard_map/all_gather | solution.py:160
  38.1 363.9 %reduce-scatter.3.cloned.1.call-start = ((), (), s32[]{:S(2)}) async-start(), calls=%async_computation.4 | async-start | bytes 5898240 | tf_op jit(solution)/shard_map/reduce_scatter | solution.py:206
  151.7 21.6 %slice-start.3 = ((s8[4718592]{0:T(1024)(128)(4,1)}), s8[4194304]{0:T(1024)(128)(4,1)S(1)}, s32[]{:S(2)}) async-start(s8[4718592]{0:T(1024)(128)(4,1)} %bitcast.233), calls=%async_computation.10 | async-start | bytes 8388608
  212.1 13.3 slice-start.2
  212.1 13.3 copy-start.7
  265.4 13.3 slice-start.2
  265.4 13.3 copy-start.7
  318.6 13.3 slice-start.2
  318.6 13.3 copy-start.7
  354.0 98.4 %reduce-scatter.5.cloned.1.call-start = ((), (), s32[]{:S(2)}) async-start(), calls=%async_computation.5 | async-start | bytes 5898240 | tf_op jit(solution)/shard_map/reduce_scatter | solution.py:209
  354.6 1273.1 %all-gather.9.cloned.1.call-start = ((), (), s32[]{:S(2)}) async-start(), calls=%async_computation.6 | async-start | bytes 31680000 | tf_op jit(solution)/shard_map/all_gather | solution.py:260
  406.9 45.5 %copy-start.38 = (f32[3,768]{1,0:T(4,128)S(1)}, f32[3,768]{1,0:T(4,128)}, u32[]{:S(2)}) copy-start(f32[3,768]{1,0:T(4,128)} %copy-done.37) | copy-start | bytes 27652
  406.9 45.5 %copy-start.43 = (f32[3,256]{1,0:T(4,128)S(1)}, f32[3,256]{1,0:T(4,128)}, u32[]{:S(2)}) copy-start(f32[3,256]{1,0:T(4,128)} %copy-done.42) | copy-start | bytes 9220
  486.0 60.7 %copy-start.17 = (f32[589824]{0:T(1024)S(1)}, f32[589824]{0:T(1024)}, u32[]{:S(2)}) copy-start(f32[589824]{0:T(1024)} %reshape.398) | copy-start | bytes 7077892
  546.7 20.2 %copy-start.60 = (f32[768]{0:T(1024)S(1)}, f32[768]{0:T(1024)}, u32[]{:S(2)}) copy-start(f32[768]{0:T(1024)} %get-tuple-element.215) | copy-start | bytes 9220
  568.1 80.4 %copy-start.65 = (f32[3072]{0:T(1024)S(1)}, f32[3072]{0:T(1024)}, u32[]{:S(2)}) copy-start(f32[3072]{0:T(1024)} %get-tuple-element.266) | copy-start | bytes 36868
  649.9 80.8 %copy-start.61 = (f32[768]{0:T(1024)S(1)}, f32[768]{0:T(1024)}, u32[]{:S(2)}) copy-start(f32[768]{0:T(1024)} %get-tuple-element.223) | copy-start | bytes 9220
  649.9 82.1 %copy-start.18 = (f32[589824]{0:T(1024)S(1)}, f32[589824]{0:T(1024)}, u32[]{:S(2)}) copy-start(f32[589824]{0:T(1024)} %reshape.401) | copy-start | bytes 7077892
  731.9 20.1 %copy-start.41 = (f32[4608]{0:T(1024)S(1)}, f32[4608]{0:T(1024)}, u32[]{:S(2)}) copy-start(f32[4608]{0:T(1024)} %get-tuple-element.303) | copy-start | bytes 55300
  1441.0 23.2 %copy-start.11 = (bf16[3,256,768]{2,1,0:T(8,128)(2,1)S(1)}, bf16[3,256,768]{2,1,0:T(8,128)(2,1)}, u32[]{:S(2)}) copy-start(bf16[3,256,768]{2,1,0:T(8,128)(2,1)} %param.18) | copy-start | bytes 3538948
  1441.0 23.2 %copy-start.13 = (f32[3,256,768]{2,1,0:T(8,128)S(1)}, f32[3,256,768]{2,1,0:T(8,128)}, u32[]{:S(2)}) copy-start(f32[3,256,768]{2,1,0:T(8,128)} %copy-done.12) | copy-start | bytes 7077892
  1441.0 23.2 %copy-start.39 = (f32[3,768]{1,0:T(4,128)S(1)}, f32[3,768]{1,0:T(4,128)}, u32[]{:S(2)}) copy-start(f32[3,768]{1,0:T(4,128)} %copy-done.37) | copy-start | bytes 27652
  1441.0 23.2 %copy-start.44 = (f32[3,256]{1,0:T(4,128)S(1)}, f32[3,256]{1,0:T(4,128)}, u32[]{:S(2)}) copy-start(f32[3,256]{1,0:T(4,128)} %copy-done.42) | copy-start | bytes 9220
  (82 other events, 464.7 us)
Sparse Core Ops, SparseCore 0:
  20.0 40.1 all-gather.4
  62.3 38.0 all-gather.6
  354.1 47.8 reduce-scatter.2
  404.5 47.8 reduce-scatter.4
  1448.9 178.7 all-gather.8
where the time goes:
time: 1880 us; the launch traced here: 1850 us
  local copies, waits for them, and re-layouts  820 us (44%)
  blocking collectives  506 us (27%)
  waiting for transfers between devices  253 us (13%)
  matrix products  185 us (10%)
  other arithmetic  71.5 us (4%)
    unnamed x1, blocking collectives  494 us
    unnamed x154, local copies, waits for them, and re-layouts  310 us
    all_gather x1, waiting for transfers between devices, shards(): lax.all_gather(joint_share.astype(jnp.bfloat16), ('seq', 'batch'), axis=0...  160 us
    slice x21, local copies, waits for them, and re-layouts, shards(): results.append(summed[cursor:cursor + element_count].reshape(tensor.shape))  104 us
    reshape x2, local copies, waits for them, and re-layouts, shards(): spread_flat = flat.reshape(share_len, shard_count).T.reshape(-1)  99.2 us
    reshape x5, local copies, waits for them, and re-layouts, shards(): results.append(summed[cursor:cursor + element_count].reshape(tensor.shape))  88.1 us
    transpose x1, local copies, waits for them, and re-layouts, shards(): spread_flat = flat.reshape(share_len, shard_count).T.reshape(-1)  72.6 us
    dynamic_slice x30, local copies, waits for them, and re-layouts, shards(): lax.map(attend, (query_low, keys_all, values_all, query_seg, key_seg))  41 us
  transfers between devices with their start and end apart: 5, of which 5 were waited for; matrix products, arithmetic and copies ran while one was open for 5% of the time, Pallas kernels for 0%

commit v1 on v0

--- a/solution.py
+++ b/solution.py
@@ -1,10 +1,13 @@
 import jax
 import jax.numpy as jnp
 from jax import lax
+from jax.experimental import pallas as pl
+from jax.experimental.pallas import tpu as pltpu
 from jax.sharding import PartitionSpec as P
 
 HEADS = 12
 HEAD = 64
+VMEM_LIMIT = 48 * 2**20
 
 
 highest = lax.Precision.HIGHEST
@@ -111,6 +114,280 @@
         key_grad.reshape(keys.shape[0], -1),
         value_grad.reshape(keys.shape[0], -1),
     )
+
+
+def swap(values, axis, bit):
+    count = lax.axis_size(axis)
+    return lax.ppermute(values, axis, [(i, i ^ bit) for i in range(count)])
+
+
+def bit_of(axis, bit):
+    return (lax.axis_index(axis) // bit) % 2
+
+
+def batch_bits():
+    count = lax.axis_size("batch")
+    bits = []
+    bit = 1
+    while bit < count:
+        bits.append(bit)
+        bit *= 2
+    return bits
+
+
+def split_orders():
+    bits = batch_bits()
+    chip = ("seq", 2)
+    split = [("batch", b) for b in bits[:3]]
+    rest = [("batch", b) for b in bits[3:]]
+    return ([chip] + split, split[:1] + [chip] + split[1:], rest)
+
+
+def position_in(order):
+    place = jnp.int32(0)
+    for axis, bit in order:
+        place = place * 2 + bit_of(axis, bit)
+    return place
+
+
+def total_of(parts):
+    total = parts[0].astype(jnp.float32)
+    for part in parts[1:]:
+        total = total + part.astype(jnp.float32)
+    return total.astype(jnp.bfloat16)
+
+
+def scatter_group(first, second, order, rest):
+    parts = [(first, 0), (second, 0)]
+    rows = first.shape[0]
+    for axis, bit in order:
+        rows //= 2
+        mine = bit_of(axis, bit)
+        send = total_of(
+            [lax.dynamic_slice_in_dim(p, at + (1 - mine) * rows, rows, 0) for p, at in parts]
+        )
+        parts = [(p, at + mine * rows) for p, at in parts] + [(swap(send, axis, bit), 0)]
+    held = total_of([lax.dynamic_slice_in_dim(p, at, rows, 0) for p, at in parts])
+    for axis, bit in rest:
+        held = total_of([held, swap(held, axis, bit)])
+    return held
+
+
+def gather_group(held, order):
+    blocks = held[None]
+    for axis, bit in reversed(order):
+        blocks = jnp.concatenate([blocks, swap(blocks, axis, bit)], axis=0)
+    return blocks
+
+
+def sync_piece(send, keep):
+    order_a, order_b, rest = split_orders()
+    got = swap(send, "seq", 1)
+    out = []
+    for g, order in ((0, order_a), (1, order_b)):
+        held = scatter_group(keep[g], got[g], order, rest)
+        full = gather_group(held, order)
+        out.append((full, swap(full, "seq", 1)))
+    (own_a, far_a), (own_b, far_b) = out
+    return own_a, own_b, far_a, far_b
+
+
+def place_scalars():
+    order_a, order_b, _ = split_orders()
+    return jnp.stack(
+        [lax.axis_index("seq") % 2, position_in(order_a), position_in(order_b)]
+    ).astype(jnp.int32)
+
+
+def chunk_at(step, core):
+    return jnp.where(step < 2, 2 * (1 - core) + step, 2 * core + step - 2)
+
+
+def weight_grad_kernel(places_ref, left_ref, right_ref, send_ref, keep_ref):
+    step = pl.program_id(0)
+    result = outer(left_ref[...], right_ref[...]).astype(jnp.bfloat16)
+
+    @pl.when(step < 2)
+    def _():
+        send_ref[0] = result
+
+    @pl.when(step >= 2)
+    def _():
+        keep_ref[0] = result
+
+
+def weight_grad(places, left, right, left_moves):
+    tokens = left.shape[0]
+    width = 768
+
+    def left_map(i, at):
+        return (0, chunk_at(i, at[0]) if left_moves else 0)
+
+    def right_map(i, at):
+        return (0, 0 if left_moves else chunk_at(i, at[0]))
+
+    return pl.pallas_call(
+        weight_grad_kernel,
+        grid_spec=pltpu.PrefetchScalarGridSpec(
+            num_scalar_prefetch=1,
+            grid=(4,),
+            in_specs=[
+                pl.BlockSpec((tokens, width), left_map),
+                pl.BlockSpec((tokens, width), right_map),
+            ],
+            out_specs=[
+                pl.BlockSpec((1, width, width), lambda i, at: (jnp.minimum(i, 1), 0, 0)),
+                pl.BlockSpec((1, width, width), lambda i, at: (jnp.maximum(i - 2, 0), 0, 0)),
+            ],
+        ),
+        out_shape=[jax.ShapeDtypeStruct((2, width, width), jnp.bfloat16)] * 2,
+        compiler_params=pltpu.CompilerParams(vmem_limit_bytes=VMEM_LIMIT),
+        cost_estimate=pl.CostEstimate(
+            flops=2 * tokens * 4 * width * width,
+            bytes_accessed=2 * (5 * tokens * width + 4 * width * width),
+            transcendentals=0,
+        ),
+    )(places, left, right)
+
+
+def attention_grad_kernel(
+    places_ref, normed_ref, merged_ref, mixed_ref, out_ref, send_ref, keep_ref
+):
+    step = pl.program_id(0)
+    chunk = chunk_at(step, places_ref[0])
+
+    def put(result):
+        @pl.when(step < 2)
+        def _():
+            send_ref[0] = result
+
+        @pl.when(step >= 2)
+        def _():
+            keep_ref[0] = result
+
+    @pl.when(chunk < 3)
+    def _():
+        put(outer(normed_ref[...], merged_ref[...]).astype(jnp.bfloat16))
+
+    @pl.when(chunk == 3)
+    def _():
+        put(outer(mixed_ref[...], out_ref[...]).astype(jnp.bfloat16))
+
+
+def attention_grad(places, normed, merged, mixed, out_low):
+    tokens = normed.shape[0]
+    width = 768
+    whole = pl.BlockSpec((tokens, width), lambda i, at: (0, 0))
+    return pl.pallas_call(
+        attention_grad_kernel,
+        grid_spec=pltpu.PrefetchScalarGridSpec(
+            num_scalar_prefetch=1,
+            grid=(4,),
+            in_specs=[
+                whole,
+                pl.BlockSpec(
+                    (tokens, width), lambda i, at: (0, jnp.minimum(chunk_at(i, at[0]), 2))
+                ),
+                whole,
+                whole,
+            ],
+            out_specs=[
+                pl.BlockSpec((1, width, width), lambda i, at: (jnp.minimum(i, 1), 0, 0)),
+                pl.BlockSpec((1, width, width), lambda i, at: (jnp.maximum(i - 2, 0), 0, 0)),
+            ],
+        ),
+        out_shape=[jax.ShapeDtypeStruct((2, width, width), jnp.bfloat16)] * 2,
+        compiler_params=pltpu.CompilerParams(vmem_limit_bytes=VMEM_LIMIT),
+        cost_estimate=pl.CostEstimate(
+            flops=2 * tokens * 4 * width * width,
+            bytes_accessed=2 * (6 * tokens * width + 4 * width * width),
+            transcendentals=0,
+        ),
+    )(places, normed, merged, mixed, out_low)
+
+
+def spread_blocks(places_ref, blocks_ref, group, out_ref):
+    count, rows, _ = blocks_ref.shape
+    for j in range(count):
+        row = pl.multiple_of((places_ref[1 + group] ^ j) * rows, 16)
+        out_ref[pl.ds(row, rows), :] = blocks_ref[j].astype(jnp.float32)
+
+
+def finish_kernel(places_ref, own_a, own_b, far_a, far_b, out_ref):
+    step = pl.program_id(0)
+    for k, (ref, group) in enumerate(((own_a, 0), (own_b, 1), (far_a, 0), (far_b, 1))):
+
+        @pl.when(step == k)
+        def _(ref=ref, group=group):
+            spread_blocks(places_ref, ref, group, out_ref)
+
+
+def finish_two_kernel(places_ref, own_a, own_b, far_a, far_b, merged_ref, out_ref):
+    step = pl.program_id(0)
+    chunk = chunk_at(step, 1 - places_ref[0])
+    for k, (ref, group) in enumerate(((own_a, 0), (own_b, 1), (far_a, 0), (far_b, 1))):
+
+        @pl.when((step == k) & (chunk < 3))
+        def _(ref=ref, group=group):
+            spread_blocks(places_ref, ref, group, merged_ref)
+
+        @pl.when((step == k) & (chunk == 3))
+        def _(ref=ref, group=group):
+            spread_blocks(places_ref, ref, group, out_ref)
+
+
+def finish_piece(places, pieces, kind):
+    count, rows, width = pieces[0].shape
+    whole = pl.BlockSpec((count, rows, width), lambda i, at: (0, 0, 0))
+    side = count * rows
+
+    def own_first(i, at):
+        return chunk_at(i, 1 - at[0])
+
+    if kind == "rows":
+        kernel = finish_kernel
+        out_specs = pl.BlockSpec((side, width), lambda i, at: (own_first(i, at), 0))
+        out_shape = jax.ShapeDtypeStruct((4 * side, width), jnp.float32)
+    elif kind == "columns":
+        kernel = finish_kernel
+        out_specs = pl.BlockSpec((side, width), lambda i, at: (0, own_first(i, at)))
+        out_shape = jax.ShapeDtypeStruct((side, 4 * width), jnp.float32)
+    else:
+        kernel = finish_two_kernel
+        out_specs = [
+            pl.BlockSpec((side, width), lambda i, at: (0, jnp.minimum(own_first(i, at), 2))),
+            pl.BlockSpec((side, width), lambda i, at: (0, 0)),
+        ]
+        out_shape = [
+            jax.ShapeDtypeStruct((side, 3 * width), jnp.float32),
+            jax.ShapeDtypeStruct((side, width), jnp.float32),
+        ]
+    return pl.pallas_call(
+        kernel,
+        grid_spec=pltpu.PrefetchScalarGridSpec(
+            num_scalar_prefetch=1, grid=(4,), in_specs=[whole] * 4, out_specs=out_specs
+        ),
+        out_shape=out_shape,
+        compiler_params=pltpu.CompilerParams(vmem_limit_bytes=VMEM_LIMIT),
+        cost_estimate=pl.CostEstimate(
+            flops=0, bytes_accessed=6 * 4 * side * width, transcendentals=0
+        ),
+    )(places, *pieces)
+
+
+def sum_small(vectors, mod_rows, cond):
+    rows = vectors.shape[0]
+    both = jnp.concatenate([vectors, mod_rows.reshape(-1, vectors.shape[1])], axis=0)
+    for bit in (1, 2):
+        both = both + swap(both, "seq", bit)
+    vectors, own = both[:rows], both[rows:]
+    everyone, conds = own, cond
+    for bit in batch_bits():
+        got = swap(jnp.concatenate([vectors, everyone], axis=0), "batch", bit)
+        vectors = vectors + got[:rows]
+        everyone = jnp.concatenate([everyone, got[rows:]], axis=0)
+        conds = jnp.concatenate([conds, swap(conds, "batch", bit)], axis=0)
+    return vectors, own.reshape(cond.shape[0], -1), everyone.reshape(conds.shape[0], -1), conds
 
 
 def shards(
@@ -130,6 +407,7 @@
     cotangent,
 ):
     row_count, span_len, features = hidden.shape
+    places = place_scalars()
     full_len = span_len * lax.axis_size("seq")
     offset = lax.axis_index("seq") * span_len
     query_seg, query_place = doc_layout(lengths, offset + jnp.arange(span_len, dtype=jnp.int32))
@@ -179,28 +457,23 @@
     gate_two_grad = jnp.sum(upstream * branch, axis=1)
     branch_grad = gate_two * upstream
     branch_low = branch_grad.astype(jnp.bfloat16).reshape(-1, features)
-    fc2_grad = outer(active_low, branch_low)
+    fc2_pieces = sync_piece(*weight_grad(places, active_low, branch_low, True))
     fc2_bias_grad = jnp.sum(branch_grad, axis=(0, 1))
     active_grad = against(branch_low, w_fc2)
     pre_grad = gelu_back(active_grad)[0]
     pre_low = pre_grad.astype(jnp.bfloat16)
     fc1_bias_grad = jnp.sum(pre_grad, axis=0)
-    fc1_grad = outer(second_low, pre_low)
+    fc1_pieces = sync_piece(*weight_grad(places, second_low, pre_low, False))
     second_grad = against(pre_low, w_fc1).reshape(row_count, span_len, features)
     resid_part, gain_two_grad, shift_two_grad, scale_two_grad = norm_two_back(second_grad)
     resid_grad = upstream + resid_part
     gate_one_grad = jnp.sum(resid_grad * attended, axis=1)
     attended_low = (gate_one * resid_grad).astype(jnp.bfloat16).reshape(-1, features)
-    out_grad = outer(mixed_low.reshape(-1, features), attended_low)
     mixed_grad = (
         against(attended_low, w_out).astype(jnp.bfloat16).reshape(row_count, span_len, features)
     )
-    keys_back, values_back = (
-        lax.all_gather(key_low, "seq", axis=1, tiled=True),
-        lax.all_gather(value_low, "seq", axis=1, tiled=True),
-    )
     query_grad, key_grad_all, value_grad_all = lax.map(
-        attend_back, (query_low, keys_back, values_back, mixed_grad, logsum, query_seg, key_seg)
+        attend_back, (query_low, keys_all, values_all, mixed_grad, logsum, query_seg, key_seg)
     )
     key_grad, value_grad = (
         lax.psum_scatter(
@@ -216,7 +489,15 @@
         .astype(jnp.bfloat16)
         .reshape(-1, 3 * features)
     )
-    qkv_grad = outer(normed_low.reshape(-1, features), merged_grad)
+    att_pieces = sync_piece(
+        *attention_grad(
+            places,
+            normed_low.reshape(-1, features),
+            merged_grad,
+            mixed_low.reshape(-1, features),
+            attended_low,
+        )
+    )
     normed_grad = against(merged_grad, w_qkv).reshape(row_count, span_len, features)
     input_part, gain_one_grad, shift_one_grad, scale_one_grad = norm_one_back(normed_grad)
     hidden_grad = (resid_grad + input_part).astype(jnp.bfloat16)
@@ -231,56 +512,35 @@
         ],
         axis=1,
     )
-    ada_grad = jnp.dot(cond.T, mod_local, precision=highest, preferred_element_type=jnp.float32)
-    ada_bias_grad = jnp.sum(mod_local, axis=0)
-    mod_total = lax.psum(mod_local.astype(jnp.bfloat16), "seq").astype(jnp.float32)
+    vectors = jnp.concatenate(
+        [
+            gain_one_grad[None],
+            gain_two_grad[None],
+            fc1_bias_grad.reshape(-1, features),
+            fc2_bias_grad[None],
+        ],
+        axis=0,
+    )
+    vectors, mod_total, mod_all, cond_all = sum_small(vectors, mod_local, cond)
+    ada_grad = jnp.dot(cond_all.T, mod_all, precision=highest, preferred_element_type=jnp.float32)
     cond_grad = jnp.dot(
         mod_total, ada_full.T, precision=highest, preferred_element_type=jnp.float32
     )
-    grad_list = [
-        gain_one_grad,
-        qkv_grad,
-        out_grad,
-        gain_two_grad,
-        fc1_grad,
-        fc1_bias_grad,
-        fc2_grad,
-        fc2_bias_grad,
-        ada_grad,
-        ada_bias_grad,
-    ]
-    flat = jnp.concatenate([tensor.reshape(-1) for tensor in grad_list])
-    shard_count = lax.axis_size("seq") * lax.axis_size("batch")
-    unit_len = 128 * shard_count
-    padded_len = -(-flat.shape[0] // unit_len) * unit_len
-    flat = jnp.pad(flat, (0, padded_len - flat.shape[0]))
-    share_len = padded_len // shard_count
-    spread_flat = flat.reshape(share_len, shard_count).T.reshape(-1)
-    joint_share = lax.psum_scatter(spread_flat, ("seq", "batch"), scatter_dimension=0, tiled=True)
-    gathered = lax.all_gather(
-        joint_share.astype(jnp.bfloat16), ("seq", "batch"), axis=0, tiled=True
-    ).astype(joint_share.dtype)
-    summed = gathered.reshape(shard_count, share_len).T.reshape(-1)
-    results = []
-    cursor = 0
-    for tensor in grad_list:
-        element_count = tensor.size
-        results.append(summed[cursor : cursor + element_count].reshape(tensor.shape))
-        cursor = cursor + element_count
+    qkv_grad, out_grad = finish_piece(places, att_pieces, "both")
     return (
         output,
         hidden_grad,
         cond_grad,
-        results[0],
-        results[1],
-        results[2],
-        results[3],
-        results[4],
-        results[5],
-        results[6],
-        results[7],
-        results[8],
-        results[9],
+        vectors[0],
+        qkv_grad,
+        out_grad,
+        vectors[1],
+        finish_piece(places, fc1_pieces, "columns"),
+        vectors[2 : 2 + w_fc1.shape[1] // features].reshape(-1),
+        finish_piece(places, fc2_pieces, "rows"),
+        vectors[-1],
+        ada_grad,
+        jnp.sum(mod_all, axis=0),
     )
 
 

time: 1880 us -> 716 us (0.38); the launches traced: 1850 us -> 707 us
  local copies, waits for them, and re-layouts: 820 us -> 186 us
  blocking collectives: 506 us -> 0 us
  waiting for transfers between devices: 253 us -> 124 us
  starting transfers between devices: 0.82 us -> 73 us
  other arithmetic: 71.5 us -> 121 us
  Pallas kernels: 0 us -> 47.4 us
  matrix products: 185 us -> 139 us
    unnamed x1 -> x0, blocking collectives: 494 us -> none
    unnamed x154 -> x203, local copies, waits for them, and re-layouts: 310 us -> 30 us
    reshape x11 -> x5, local copies, waits for them, and re-layouts: 212 us -> 6.91 us  [the longest x1 1.9 us: sum_small(): everyone.reshape(conds.shape[0], -1)]
    all_gather x1 -> x0, waiting for transfers between devices: 160 us -> none  [shards(): lax.all_gather(joint_share.astype(jnp.bfloat16), ('seq', 'batch'), axis=0...]
    slice x21 -> x12, local copies, waits for them, and re-layouts: 104 us -> 13.5 us  [the longest x6 10.4 us: sync_piece(): held = scatter_group(keep[g], got[g], order, rest)]
    ppermute x0 -> x65, waiting for transfers between devices: none -> 72.9 us  [swap(): return lax.ppermute(values, axis, [(i, i ^ bit) for i in range(count)])]
    ppermute x0 -> x65, starting transfers between devices: none -> 72.6 us  [swap(): return lax.ppermute(values, axis, [(i, i ^ bit) for i in range(count)])]
    transpose x1 -> x0, local copies, waits for them, and re-layouts: 72.6 us -> none  [shards(): spread_flat = flat.reshape(share_len, shard_count).T.reshape(-1)]
  transfers between devices with their start and end apart: 5 -> 69, of which waited for: 5 -> 23; matrix products, arithmetic and copies ran while one was open for 5% -> 26% of each run, Pallas kernels for 0% -> 6%
where the time goes in v1:
time: 716 us; the launch traced here: 707 us
  local copies, waits for them, and re-layouts  186 us (26%)
  matrix products  139 us (19%)
  waiting for transfers between devices  124 us (17%)
  other arithmetic  121 us (17%)
  starting transfers between devices  73 us (10%)
  Pallas kernels  47.4 us (7%)
  between operations  15.5 us (2%)
    ppermute x65, waiting for transfers between devices, swap(): return lax.ppermute(values, axis, [(i, i ^ bit) for i in range(count)])  72.9 us
    ppermute x65, starting transfers between devices, swap(): return lax.ppermute(values, axis, [(i, i ^ bit) for i in range(count)])  72.6 us
    dynamic_slice x30, local copies, waits for them, and re-layouts, shards(): lax.map(attend, (query_low, keys_all, values_all, query_seg, key_seg))  42.7 us
    all_gather x1, waiting for transfers between devices, shards(): lax.all_gather(key_low, 'seq', axis=1, tiled=True)  33.6 us
    dot_general x3, matrix products, attend_back(): jnp.einsum('chd,khd->hck', grad_heads, value_heads, preferred_element_typ...  33 us
    unnamed x203, local copies, waits for them, and re-layouts  30 us
    convert_element_type x24, other arithmetic, total_of(): return total.astype(jnp.bfloat16)  26.9 us
    dot_general x4, matrix products, against(): lax.dot_general(values, weight, (((1,), (1,)), ((), ())), preferred_eleme...  25.8 us
  transfers between devices with their start and end apart: 69, of which 23 were waited for; matrix products, arithmetic and copies ran while one was open for 26% of the time, Pallas kernels for 6%

profile of v1, /device:TPU:0, one launch (start us, length us, event | category | flops | bytes accessed | tf_op | source)
XLA Modules:
  0.0 707.0 jit_solution(9349382340441634066)
XLA Ops:
  45.8 17.6 %all-gather.3.cloned.1.call-done = bf16[3,1024,768]{2,1,0:T(8,128)(2,1)} async-done(((bf16[3,256,768]{2,1,0:T(8,128)(2,1)}), bf16[3,1024,768]{2,1,0:T(8,128)(2,1)}) %all-gather.3.cloned.1.call-update) | async-done | bytes 4718608 | tf_op jit(solution)/shard_map/all_gather | solution.py:439
  63.4 6.6 copy.55
  70.0 33.6 %all-gather.5.cloned.1.call-done = bf16[3,1024,768]{1,2,0:T(8,128)(2,1)} async-done(((bf16[3,256,768]{1,2,0:T(8,128)(2,1)}), bf16[3,1024,768]{1,2,0:T(8,128)(2,1)}) %all-gather.5.cloned.1.call-update) | async-done | bytes 4718608 | tf_op jit(solution)/shard_map/all_gather | solution.py:438
  103.6 48.7 %while.28 = (s32[]{:T(128)}, bf16[3,256,768]{1,2,0:T(8,128)(2,1)}, f32[3,12,256]{2,1,0:T(8,128)}, bf16[3,1024,768]{1,2,0:T(8,128)(2,1)}, s32[3,256]{1,0:T(4,128)...) while((s32[]{:T(128)}, bf16[3,256,768]{1,2,0:T(8,128)(2,1)}, ...), condition=%wide.region_9.10_spmd.clone, body=%wide.region_6.9_spmd.sunk.clone | while | flops 843314176 | bytes 50711668 | solution.py:441
  158.6 9.6 %fusion.151 = f32[768,3072]{1,0:T(8,128)} fusion(bf16[768,768]{1,0:T(8,128)(2,1)S(1)} %bitcast.398, bf16[768,3072]{1,0:T(8,128)(2,1)} %param.25), kind=kOutput, calls=%fused_computation.323 | convolution fusion | flops 3623878656 | bytes 15335424 | tf_op jit(solution)/shard_map/dot_general | solution.py:449
  168.2 14.2 %fusion.138 = (f32[3072]{0:T(1024)}, bf16[768,3072]{1,0:T(8,128)(2,1)S(1)}, bf16[768,3072]{1,0:T(8,128)(2,1)}) fusion(f32[768,3072]{1,0:T(8,128)} %fusion.151, f32[3072]{0:T(1024)S(1)} %copy-done.89, bf16[768,768]{1,0:T(8,128)(2,1)S(1)} %bitcast.396, bf16[3072,768]{1,0:T(8,128)(2,1)S(1)} %bitcast.436), kind=kOutput, calls=%fused_computation.310 | convolution fusion | flops 3680498688 | bytes 24797184 | tf_op jit(solution)/shard_map/dot_general | solution.py:61
  193.5 147.2 %while.29 = (s32[]{:T(128)}, f32[3,256,768]{1,2,0:T(8,128)}, bf16[3,1024,768]{1,2,0:T(8,128)(2,1)}, bf16[3,1024,768]{2,1,0:T(8,128)(2,1)}, bf16[3,1024,768]{1,2,...) while((s32[]{:T(128)}, f32[3,256,768]{1,2,0:T(8,128)}, ...), condition=%wide.region_16.17_spmd.clone, body=%wide.region_14.16_spmd.sunk.clone | while | flops 2062480384 | bytes 232984080 | solution.py:475
  219.3 11.0 %multiply_reduce_fusion.8 = (f32[12,256]{1,0:T(8,128)S(1)}, f32[12,256,1024]{2,1,0:T(8,128)}) fusion(f32[12,256,1024]{2,1,0:T(8,128)} %copy-done.13, f32[12,256]{1,0:T(8,128)} %dynamic-slice_bitcast_fusion.3, pred[256,1024]{1,0:T(8,128)(4,1)} %broadcast_compare_fusion.7, bf16[256,12,64]{0,2,1:T(8,128)(2,1)} %bitcast.413, ...), kind=kOutput, calls=%fused_computation.17.clone.1.clone | convolution fusion | flops 418378752 | bytes 27418624 | tf_op jit(solution)/shard_map/while/body/eval_jaxpr/chd,khd->hck/dot_general | solution.py:100
  230.4 6.9 multiply_convert_fusion.5
  268.2 11.0 %multiply_reduce_fusion.8 = (f32[12,256]{1,0:T(8,128)S(1)}, f32[12,256,1024]{2,1,0:T(8,128)}) fusion(f32[12,256,1024]{2,1,0:T(8,128)} %copy-done.13, f32[12,256]{1,0:T(8,128)} %dynamic-slice_bitcast_fusion.3, pred[256,1024]{1,0:T(8,128)(4,1)} %broadcast_compare_fusion.7, bf16[256,12,64]{0,2,1:T(8,128)(2,1)} %bitcast.413, ...), kind=kOutput, calls=%fused_computation.17.clone.1.clone | convolution fusion | flops 418378752 | bytes 27418624 | tf_op jit(solution)/shard_map/while/body/eval_jaxpr/chd,khd->hck/dot_general | solution.py:100
  279.3 6.9 multiply_convert_fusion.5
  317.1 11.0 %multiply_reduce_fusion.8 = (f32[12,256]{1,0:T(8,128)S(1)}, f32[12,256,1024]{2,1,0:T(8,128)}) fusion(f32[12,256,1024]{2,1,0:T(8,128)} %copy-done.13, f32[12,256]{1,0:T(8,128)} %dynamic-slice_bitcast_fusion.3, pred[256,1024]{1,0:T(8,128)(4,1)} %broadcast_compare_fusion.7, bf16[256,12,64]{0,2,1:T(8,128)(2,1)} %bitcast.413, ...), kind=kOutput, calls=%fused_computation.17.clone.1.clone | convolution fusion | flops 418378752 | bytes 27418624 | tf_op jit(solution)/shard_map/while/body/eval_jaxpr/chd,khd->hck/dot_general | solution.py:100
  328.2 6.9 multiply_convert_fusion.5
  342.2 8.8 %shard_map.241 = (bf16[2,768,768]{2,1,0:T(8,128)(2,1)}, bf16[2,768,768]{2,1,0:T(8,128)(2,1)S(1)}) custom-call(s32[3]{0:T(128)S(1)} %pad_add_fusion.places_ref, bf16[768,3072]{1,0:T(8,128)(2,1)} %get-tuple-element.273.left_ref, bf16[768,768]{1,0:T(8,128)(2,1)S(1)} %bitcast.397), custom_call_target="tpu_custom_call" | custom-call | flops 3623878656 | bytes 10616832 | tf_op jit(solution)/shard_map/pallas_call | solution.py:229
  352.6 8.3 %shard_map.239 = (bf16[2,768,768]{2,1,0:T(8,128)(2,1)}, bf16[2,768,768]{2,1,0:T(8,128)(2,1)S(1)}) custom-call(s32[3]{0:T(128)S(1)} %pad_add_fusion.places_ref, bf16[768,768]{1,0:T(8,128)(2,1)S(1)} %bitcast.399, bf16[768,3072]{1,0:T(8,128)(2,1)} %copy-done.91), custom_call_target="tpu_custom_call" | custom-call | flops 3623878656 | bytes 10616832 | tf_op jit(solution)/shard_map/pallas_call | solution.py:229
  405.2 8.0 %collective-permute-done.25 = bf16[384,768]{1,0:T(8,128)(2,1)} collective-permute-done((bf16[384,768]{1,0:T(8,128)(2,1)}, bf16[384,768]{1,0:T(8,128)(2,1)}, u32[]{:S(2)}, u32[]{:S(2)}) %collective-permute-start.25) | collective-permute-done | bytes 589856 | tf_op jit(solution)/shard_map/ppermute | solution.py:121
  486.7 6.8 collective-permute-done.59
  526.1 8.8 %shard_map.237 = (bf16[2,768,768]{2,1,0:T(8,128)(2,1)}, bf16[2,768,768]{2,1,0:T(8,128)(2,1)}) custom-call(s32[3]{0:T(128)S(1)} %pad_add_fusion.places_ref, bf16[768,768]{1,0:T(8,128)(2,1)S(1)} %bitcast.393, bf16[768,2304]{1,0:T(8,128)(2,1)} %pad_maximum_fusion.merged_ref, bf16[768,768]{1,0:T(8,128)(2,1)S(1)} %bitcast.392, bf16[768,768]{1,0:T(8,128)(2,1)S(1)} %bitcast.395), custom_call_target="tpu_custom_call" | custom-call | flops 3623878656 | bytes 11796480 | tf_op jit(solution)/shard_map/pallas_call | solution.py:281
  546.8 5.6 fusion.41
  566.2 7.5 %collective-permute-done.6 = bf16[384,768]{1,0:T(8,128)(2,1)} collective-permute-done((bf16[384,768]{1,0:T(8,128)(2,1)S(1)}, bf16[384,768]{1,0:T(8,128)(2,1)}, u32[]{:S(2)}, u32[]{:S(2)}) %collective-permute-start.6) | collective-permute-done | bytes 589856 | tf_op jit(solution)/shard_map/ppermute | solution.py:121
  595.3 6.8 shard_map.240
  602.1 7.1 %shard_map.242 = f32[3072,768]{1,0:T(8,128)} custom-call(s32[3]{0:T(128)S(1)} %pad_add_fusion.places_ref, bf16[16,48,768]{2,1,0:T(8,128)(2,1)} %constant_dynamic-update-slice_fusion.30.own_a, bf16[16,48,768]{2,1,0:T(8,128)(2,1)} %constant_dynamic-update-slice_fusion.35.own_b, bf16[16,48,768]{2,1,0:T(8,128)(2,1)} %collective-permute-done.60.far_a, ...), custom_call_target="tpu_custom_call" | custom-call | bytes 14155776 | tf_op jit(solution)/shard_map/pallas_call | solution.py:365
  670.7 11.4 %collective-permute-done.4 = f32[79,768]{1,0:T(8,128)S(1)} collective-permute-done((f32[79,768]{1,0:T(8,128)S(1)}, f32[79,768]{1,0:T(8,128)S(1)}, u32[]{:S(2)}, u32[]{:S(2)}) %collective-permute-start.4) | collective-permute-done | bytes 242720 | tf_op jit(solution)/shard_map/ppermute | solution.py:121
  692.3 7.6 %shard_map.238 = (f32[768,2304]{1,0:T(8,128)}, f32[768,768]{1,0:T(8,128)}) custom-call(s32[3]{0:T(128)S(1)} %pad_add_fusion.places_ref, bf16[16,48,768]{2,1,0:T(8,128)(2,1)} %constant_dynamic-update-slice_fusion.10.own_a, bf16[16,48,768]{2,1,0:T(8,128)(2,1)} %constant_dynamic-update-slice_fusion.15.own_b, ...), custom_call_target="tpu_custom_call" | custom-call | bytes 14155776 | tf_op jit(solution)/shard_map/pallas_call | solution.py:365
  (648 shorter events, 468.5 us)
Async XLA Ops:
  7.2 56.2 %all-gather.3.cloned.1.call-start = ((), (), s32[]{:S(2)}) async-start(), calls=%async_computation.2 | async-start | bytes 5898240 | tf_op jit(solution)/shard_map/all_gather | solution.py:439
  23.1 80.5 %all-gather.5.cloned.1.call-start = ((), (), s32[]{:S(2)}) async-start(), calls=%async_computation.3 | async-start | bytes 5898240 | tf_op jit(solution)/shard_map/all_gather | solution.py:438
  41.3 453.0 %reduce-scatter.3.cloned.1.call-start = ((), (), s32[]{:S(2)}) async-start(), calls=%async_computation.4 | async-start | bytes 5898240 | tf_op jit(solution)/shard_map/reduce_scatter | solution.py:479
  340.7 181.4 %reduce-scatter.5.cloned.1.call-start = ((), (), s32[]{:S(2)}) async-start(), calls=%async_computation.5 | async-start | bytes 5898240 | tf_op jit(solution)/shard_map/reduce_scatter | solution.py:482
  352.3 19.2 %collective-permute-start.43 = (bf16[2,768,768]{2,1,0:T(8,128)(2,1)}, bf16[2,768,768]{2,1,0:T(8,128)(2,1)}, u32[]{:S(2)}, u32[]{:S(2)}) collective-permute-start(bf16[2,768,768]{2,1,0:T(8,128)(2,1)} %get-tuple-element.135), channel_id=1, source_target_pairs={{0,8},{8,0},{16,24},{24,16},{1,9},{9,1},{17,25},{25,17},{2,10},{10... | collective-permute-start | bytes 7077896 | tf_op jit(solution)/shard_map/ppermute | solution.py:121
  367.4 197.1 %collective-permute-start.63 = (f32[6,128]{1,0:T(8,128)}, f32[6,128]{1,0:T(8,128)}, u32[]{:S(2)}, u32[]{:S(2)}) collective-permute-start(f32[6,128]{1,0:T(8,128)} %pad_maximum_fusion.25), channel_id=1, source_target_pairs={{0,2},{1,3},{2,0},{3,1},{4,6},{5,7},{6,4},{7,5},{8,10},{9,11},{10,... | collective-permute-start | bytes 9224 | tf_op jit(solution)/shard_map/ppermute | solution.py:121
  376.3 24.2 %collective-permute-start.44 = (bf16[384,768]{1,0:T(8,128)(2,1)}, bf16[384,768]{1,0:T(8,128)(2,1)}, u32[]{:S(2)}, u32[]{:S(2)}) collective-permute-start(bf16[384,768]{1,0:T(8,128)(2,1)} %fusion.50), channel_id=1, source_target_pairs={{0,16},{8,24},{16,0},{24,8},{1,17},{9,25},{17,1},{25,9},{2,18},{10... | collective-permute-start | bytes 1769480 | tf_op jit(solution)/shard_map/ppermute | solution.py:121
  377.8 25.5 %collective-permute-start.52 = (bf16[384,768]{1,0:T(8,128)(2,1)}, bf16[384,768]{1,0:T(8,128)(2,1)}, u32[]{:S(2)}, u32[]{:S(2)}) collective-permute-start(bf16[384,768]{1,0:T(8,128)(2,1)} %fusion.51), channel_id=1, source_target_pairs={{0,1},{1,0},{2,3},{3,2},{4,5},{5,4},{6,7},{7,6},{8,9},{9,8},{10,11... | collective-permute-start | bytes 1769480 | tf_op jit(solution)/shard_map/ppermute | solution.py:121
  382.2 30.9 %collective-permute-start.25 = (bf16[384,768]{1,0:T(8,128)(2,1)}, bf16[384,768]{1,0:T(8,128)(2,1)}, u32[]{:S(2)}, u32[]{:S(2)}) collective-permute-start(bf16[384,768]{1,0:T(8,128)(2,1)} %fusion.48), channel_id=1, source_target_pairs={{0,16},{8,24},{16,0},{24,8},{1,17},{9,25},{17,1},{25,9},{2,18},{10... | collective-permute-start | bytes 1769480 | tf_op jit(solution)/shard_map/ppermute | solution.py:121
  384.8 31.1 %collective-permute-start.33 = (bf16[384,768]{1,0:T(8,128)(2,1)}, bf16[384,768]{1,0:T(8,128)(2,1)}, u32[]{:S(2)}, u32[]{:S(2)}) collective-permute-start(bf16[384,768]{1,0:T(8,128)(2,1)} %fusion.49), channel_id=1, source_target_pairs={{0,1},{1,0},{2,3},{3,2},{4,5},{5,4},{6,7},{7,6},{8,9},{9,8},{10,11... | collective-permute-start | bytes 1769480 | tf_op jit(solution)/shard_map/ppermute | solution.py:121
  475.5 63.8 %collective-permute-start.51 = (bf16[8,48,768]{2,1,0:T(8,128)(2,1)}, bf16[8,48,768]{2,1,0:T(8,128)(2,1)}, u32[]{:S(2)}, u32[]{:S(2)}) collective-permute-start(bf16[8,48,768]{2,1,0:T(8,128)(2,1)} %pad_maximum_fusion.7), channel_id=1, source_target_pairs={{0,16},{8,24},{16,0},{24,8},{1,17},{9,25},{17,1},{25,9},{2,18},{10... | collective-permute-start | bytes 1769480 | tf_op jit(solution)/shard_map/ppermute | solution.py:121
  479.5 57.8 %collective-permute-start.32 = (bf16[8,48,768]{2,1,0:T(8,128)(2,1)}, bf16[8,48,768]{2,1,0:T(8,128)(2,1)}, u32[]{:S(2)}, u32[]{:S(2)}) collective-permute-start(bf16[8,48,768]{2,1,0:T(8,128)(2,1)} %pad_maximum_fusion.5), channel_id=1, source_target_pairs={{0,16},{8,24},{16,0},{24,8},{1,17},{9,25},{17,1},{25,9},{2,18},{10... | collective-permute-start | bytes 1769480 | tf_op jit(solution)/shard_map/ppermute | solution.py:121
  482.2 52.7 %collective-permute-start.40 = (bf16[8,48,768]{2,1,0:T(8,128)(2,1)}, bf16[8,48,768]{2,1,0:T(8,128)(2,1)}, u32[]{:S(2)}, u32[]{:S(2)}) collective-permute-start(bf16[8,48,768]{2,1,0:T(8,128)(2,1)} %pad_maximum_fusion.6), channel_id=1, source_target_pairs={{0,1},{1,0},{2,3},{3,2},{4,5},{5,4},{6,7},{7,6},{8,9},{9,8},{10,11... | collective-permute-start | bytes 1769480 | tf_op jit(solution)/shard_map/ppermute | solution.py:121
  494.3 107.8 %collective-permute-start.61 = (bf16[16,48,768]{2,1,0:T(8,128)(2,1)}, bf16[16,48,768]{2,1,0:T(8,128)(2,1)}, u32[]{:S(2)}, u32[]{:S(2)}) collective-permute-start(bf16[16,48,768]{2,1,0:T(8,128)(2,1)} %constant_dynamic-update-slice_fusion.35.own_b), channel_id=1, source_target_pairs={{0,8},{8,0},{16,24},{24,16},{1,9},{9,1},{17,25},{25,17},{2,10},{10... | collective-permute-start | bytes 3538952 | tf_op jit(solution)/shard_map/ppermute | solution.py:121
  534.9 19.6 %collective-permute-start.5 = (bf16[2,768,768]{2,1,0:T(8,128)(2,1)}, bf16[2,768,768]{2,1,0:T(8,128)(2,1)}, u32[]{:S(2)}, u32[]{:S(2)}) collective-permute-start(bf16[2,768,768]{2,1,0:T(8,128)(2,1)} %get-tuple-element.129), channel_id=1, source_target_pairs={{0,8},{8,0},{16,24},{24,16},{1,9},{9,1},{17,25},{25,17},{2,10},{10... | collective-permute-start | bytes 7077896 | tf_op jit(solution)/shard_map/ppermute | solution.py:121
  537.3 48.5 %collective-permute-start.42 = (bf16[16,48,768]{2,1,0:T(8,128)(2,1)}, bf16[16,48,768]{2,1,0:T(8,128)(2,1)}, u32[]{:S(2)}, u32[]{:S(2)}) collective-permute-start(bf16[16,48,768]{2,1,0:T(8,128)(2,1)} %constant_dynamic-update-slice_fusion.25.own_b), channel_id=1, source_target_pairs={{0,8},{8,0},{16,24},{24,16},{1,9},{9,1},{17,25},{25,17},{2,10},{10... | collective-permute-start | bytes 3538952 | tf_op jit(solution)/shard_map/ppermute | solution.py:121
  539.3 53.1 %collective-permute-start.41 = (bf16[16,48,768]{2,1,0:T(8,128)(2,1)}, bf16[16,48,768]{2,1,0:T(8,128)(2,1)}, u32[]{:S(2)}, u32[]{:S(2)}) collective-permute-start(bf16[16,48,768]{2,1,0:T(8,128)(2,1)} %constant_dynamic-update-slice_fusion.20.own_a), channel_id=1, source_target_pairs={{0,8},{8,0},{16,24},{24,16},{1,9},{9,1},{17,25},{25,17},{2,10},{10... | collective-permute-start | bytes 3538952 | tf_op jit(solution)/shard_map/ppermute | solution.py:121
  564.6 37.5 %collective-permute-start.60 = (bf16[16,48,768]{2,1,0:T(8,128)(2,1)}, bf16[16,48,768]{2,1,0:T(8,128)(2,1)}, u32[]{:S(2)}, u32[]{:S(2)}) collective-permute-start(bf16[16,48,768]{2,1,0:T(8,128)(2,1)} %constant_dynamic-update-slice_fusion.30.own_a), channel_id=1, source_target_pairs={{0,8},{8,0},{16,24},{24,16},{1,9},{9,1},{17,25},{25,17},{2,10},{10... | collective-permute-start | bytes 3538952 | tf_op jit(solution)/shard_map/ppermute | solution.py:121
  588.4 25.1 %collective-permute-start.7 = (bf16[192,768]{1,0:T(8,128)(2,1)}, bf16[192,768]{1,0:T(8,128)(2,1)}, u32[]{:S(2)}, u32[]{:S(2)}) collective-permute-start(bf16[192,768]{1,0:T(8,128)(2,1)} %fusion.57), channel_id=1, source_target_pairs={{0,1},{1,0},{2,3},{3,2},{4,5},{5,4},{6,7},{7,6},{8,9},{9,8},{10,11... | collective-permute-start | bytes 884744 | tf_op jit(solution)/shard_map/ppermute | solution.py:121
  591.8 24.5 %collective-permute-start.15 = (bf16[192,768]{1,0:T(8,128)(2,1)}, bf16[192,768]{1,0:T(8,128)(2,1)}, u32[]{:S(2)}, u32[]{:S(2)}) collective-permute-start(bf16[192,768]{1,0:T(8,128)(2,1)} %fusion.56), channel_id=1, source_target_pairs={{0,16},{8,24},{16,0},{24,8},{1,17},{9,25},{17,1},{25,9},{2,18},{10... | collective-permute-start | bytes 884744 | tf_op jit(solution)/shard_map/ppermute | solution.py:121
  602.1 85.7 %collective-permute-start.64 = (f32[12,128]{1,0:T(8,128)}, f32[12,128]{1,0:T(8,128)}, u32[]{:S(2)}, u32[]{:S(2)}) collective-permute-start(f32[12,128]{1,0:T(8,128)} %pad_maximum_fusion.24), channel_id=1, source_target_pairs={{0,4},{1,5},{2,6},{3,7},{4,0},{5,1},{6,2},{7,3},{8,12},{9,13},{10,... | collective-permute-start | bytes 18440 | tf_op jit(solution)/shard_map/ppermute | solution.py:121
  645.0 22.5 %collective-permute-start.3 = (f32[43,768]{1,0:T(8,128)S(1)}, f32[43,768]{1,0:T(8,128)S(1)}, u32[]{:S(2)}, u32[]{:S(2)}) collective-permute-start(f32[43,768]{1,0:T(8,128)S(1)} %pad_maximum_fusion.17), channel_id=1, source_target_pairs={{0,2},{1,3},{2,0},{3,1},{4,6},{5,7},{6,4},{7,5},{8,10},{9,11},{10,... | collective-permute-start | bytes 396296 | tf_op jit(solution)/shard_map/ppermute | solution.py:121
  665.8 26.5 %collective-permute-start.23 = (bf16[16,48,768]{2,1,0:T(8,128)(2,1)}, bf16[16,48,768]{2,1,0:T(8,128)(2,1)}, u32[]{:S(2)}, u32[]{:S(2)}) collective-permute-start(bf16[16,48,768]{2,1,0:T(8,128)(2,1)} %constant_dynamic-update-slice_fusion.15.own_b), channel_id=1, source_target_pairs={{0,8},{8,0},{16,24},{24,16},{1,9},{9,1},{17,25},{25,17},{2,10},{10... | collective-permute-start | bytes 3538952 | tf_op jit(solution)/shard_map/ppermute | solution.py:121
  667.5 24.8 %collective-permute-start.22 = (bf16[16,48,768]{2,1,0:T(8,128)(2,1)}, bf16[16,48,768]{2,1,0:T(8,128)(2,1)}, u32[]{:S(2)}, u32[]{:S(2)}) collective-permute-start(bf16[16,48,768]{2,1,0:T(8,128)(2,1)} %constant_dynamic-update-slice_fusion.10.own_a), channel_id=1, source_target_pairs={{0,8},{8,0},{16,24},{24,16},{1,9},{9,1},{17,25},{25,17},{2,10},{10... | collective-permute-start | bytes 3538952 | tf_op jit(solution)/shard_map/ppermute | solution.py:121
  (174 other events, 1416.6 us)
Sparse Core Ops, SparseCore 0:
  23.2 40.1 all-gather.2
  65.5 38.0 all-gather.4
  340.8 56.2 reduce-scatter.2
  399.7 52.1 reduce-scatter.4

commit v2 on v1

v2 whole, which is shorter than its diff:
```python
import functools

import jax
import jax.numpy as jnp
from jax import lax
from jax.experimental import pallas as pl
from jax.experimental.pallas import tpu as pltpu
from jax.sharding import PartitionSpec as P

HEADS = 12
HEAD = 64
DOCS = 8
LANES = 128
GELU_A = 0.7978845608
GELU_B = 0.044715
VMEM_LIMIT = 60 * 2**20


highest = lax.Precision.HIGHEST


def dot_nt(left, right):
    return lax.dot_general(
        left, right, (((1,), (1,)), ((), ())), preferred_element_type=jnp.float32
    )


def dot_tn(left, right):
    return lax.dot_general(
        left, right, (((0,), (0,)), ((), ())), preferred_element_type=jnp.float32
    )


def dot_nn(left, right):
    return jnp.dot(left, right, preferred_element_type=jnp.float32)


def column_sum(values):
    return jnp.sum(values, axis=0, keepdims=True)


def row_mean(values):
    return jnp.mean(values, axis=-1, keepdims=True)


def normalized(values):
    center = values - row_mean(values)
    inverse = lax.rsqrt(row_mean(center * center) + 1e-05)
    return center * inverse, inverse


def documents_of(slots, layout_ref, group):
    end = jnp.int32(0)
    segment = jnp.zeros_like(slots)
    start = jnp.zeros_like(slots)
    for i in range(DOCS):
        length = layout_ref[group * DOCS + i]
        end = end + length
        passed = slots >= end
        segment = segment + passed.astype(jnp.int32)
        start = start + jnp.where(passed, length, 0)
    return segment, slots - start


def base_of(layout_ref, block):
    return layout_ref[2 * DOCS + block]


def turned(values, cosine, sine):
    lanes = lax.broadcasted_iota(jnp.int32, cosine.shape, 1)
    first = lanes % HEAD < HEAD // 2
    pieces = []
    for c in range(values.shape[1] // LANES):
        u = values[:, c * LANES : (c + 1) * LANES]
        other = jnp.where(
            first, pltpu.roll(u, LANES - HEAD // 2, 1), pltpu.roll(u, HEAD // 2, 1)
        )
        pieces.append(u * cosine + other * sine)
    return pieces


def project_kernel(groups, bases, layout_ref, *refs):
    count = len(groups)
    hidden = refs[:count]
    mod_ref, gain_ref, speed_ref, weight_ref = refs[count : count + 4]
    normed = refs[count + 4 : 2 * count + 4]
    query = refs[2 * count + 4 : 3 * count + 4]
    keyval = refs[3 * count + 4 : 4 * count + 4]
    angle = refs[4 * count + 4 : 5 * count + 4]
    step = pl.program_id(0)
    span = hidden[0].shape[0]

    @pl.when(step == 0)
    def _():
        for b in range(count):
            values, _ = normalized(hidden[b][...].astype(jnp.float32))
            scale = mod_ref[groups[b], 1:2, :]
            shift = mod_ref[groups[b], 0:1, :]
            normed[b][...] = (values * gain_ref[...] * (1.0 + scale) + shift).astype(jnp.bfloat16)
            slots = base_of(layout_ref, bases[b]) + lax.broadcasted_iota(
                jnp.int32, (span, LANES), 0
            )
            _, place = documents_of(slots, layout_ref, groups[b])
            lanes = lax.broadcasted_iota(jnp.int32, (span, LANES), 1)
            angles = place.astype(jnp.float32) * speed_ref[...]
            sine = jnp.sin(angles)
            angle[b][0] = jnp.cos(angles)
            angle[b][1] = jnp.where(lanes % HEAD < HEAD // 2, -sine, sine)

    for b in range(count):
        merged = dot_nn(normed[b][...], weight_ref[...])

        @pl.when(step == 0)
        def _(b=b, merged=merged):
            for c, piece in enumerate(turned(merged, angle[b][0], angle[b][1])):
                query[b][:, c * LANES : (c + 1) * LANES] = (piece * 0.125).astype(jnp.bfloat16)

        @pl.when(step == 1)
        def _(b=b, merged=merged):
            for c, piece in enumerate(turned(merged, angle[b][0], angle[b][1])):
                keyval[b][c, :, :LANES] = piece.astype(jnp.bfloat16)

        @pl.when(step == 2)
        def _(b=b, merged=merged):
            for c in range(merged.shape[1] // LANES):
                keyval[b][c, :, LANES:] = merged[:, c * LANES : (c + 1) * LANES].astype(
                    jnp.bfloat16
                )


def speeds():
    half = 10000.0 ** (-jnp.arange(HEAD // 2, dtype=jnp.float32) * 2.0 / HEAD)
    return jnp.tile(half, LANES // (HEAD // 2))[None]


def project(layout, hidden, mod, gain, weight, groups, bases):
    count = len(hidden)
    span, width = hidden[0].shape
    pairs = width // LANES
    whole = pl.BlockSpec((span, width), lambda i, at: (0, 0))
    return pl.pallas_call(
        functools.partial(project_kernel, groups, bases),
        grid_spec=pltpu.PrefetchScalarGridSpec(
            num_scalar_prefetch=1,
            grid=(3,),
            in_specs=[whole] * count
            + [
                pl.BlockSpec(mod.shape, lambda i, at: (0, 0, 0)),
                pl.BlockSpec(gain.shape, lambda i, at: (0, 0)),
                pl.BlockSpec((1, LANES), lambda i, at: (0, 0)),
                pl.BlockSpec((width, width), lambda i, at: (0, i)),
            ],
            out_specs=[whole] * (2 * count)
            + [pl.BlockSpec((pairs, span, 2 * LANES), lambda i, at: (0, 0, 0))] * count
            + [pl.BlockSpec((2, span, LANES), lambda i, at: (0, 0, 0))] * count,
        ),
        out_shape=[jax.ShapeDtypeStruct((span, width), jnp.bfloat16)] * (2 * count)
        + [jax.ShapeDtypeStruct((pairs, span, 2 * LANES), jnp.bfloat16)] * count
        + [jax.ShapeDtypeStruct((2, span, LANES), jnp.float32)] * count,
        compiler_params=pltpu.CompilerParams(vmem_limit_bytes=VMEM_LIMIT),
        cost_estimate=pl.CostEstimate(
            flops=6 * count * span * width * width,
            bytes_accessed=2 * (5 * count * span * width + 3 * width * width),
            transcendentals=0,
        ),
    )(layout, *hidden, mod, gain, speeds(), weight)


def mask_into(bias_ref, layout_ref, group, query_blocks):
    span = bias_ref.shape[-1]
    rows = lax.broadcasted_iota(jnp.int32, (span, span), 0)
    columns = lax.broadcasted_iota(jnp.int32, (span, span), 1)
    for k in range(4):
        key_segment, _ = documents_of(base_of(layout_ref, k) + rows, layout_ref, group)
        for q in range(query_blocks):
            query_segment, _ = documents_of(base_of(layout_ref, q) + columns, layout_ref, group)
            bias_ref[q, k] = jnp.where(key_segment == query_segment, 0.0, -1e30)


def one_head(values, head):
    lanes = lax.broadcasted_iota(jnp.int32, values.shape, 1)
    return jnp.where(lanes // HEAD == head, values, jnp.zeros_like(values))


def attend_kernel(group, count, layout_ref, *refs):
    query = refs[:count]
    keyval = refs[count : count + 4]
    mixed = refs[count + 4 : 2 * count + 4]
    logsum = refs[2 * count + 4 : 3 * count + 4]
    bias_ref, score_ref = refs[3 * count + 4 :]

    @pl.when(pl.program_id(0) == 0)
    def _():
        mask_into(bias_ref, layout_ref, group, count)

    turned_values = [keyval[k][0, :, LANES:].T for k in range(4)]
    for q in range(count):
        heads = []
        for h in range(2):
            chosen = one_head(query[q][...], h)
            peak = None
            for k in range(4):
                scores = dot_nt(keyval[k][0, :, :LANES], chosen) + bias_ref[q, k]
                score_ref[h, k] = scores
                top = jnp.max(scores, axis=0, keepdims=True)
                peak = top if peak is None else jnp.maximum(peak, top)
            total = None
            sums = None
            for k in range(4):
                expo = jnp.exp(score_ref[h, k] - peak)
                part = jnp.sum(expo, axis=0, keepdims=True)
                total = part if total is None else total + part
                values = turned_values[k][h * HEAD : (h + 1) * HEAD, :]
                term = dot_nn(values, expo.astype(jnp.bfloat16))
                sums = term if sums is None else sums + term
            heads.append(sums / total)
            logsum[q][0, h : h + 1, :] = peak + jnp.log(total)
        mixed[q][...] = jnp.concatenate(heads, axis=0).T.astype(jnp.bfloat16)


def attend(layout, query, keyval, group):
    count = len(query)
    span, width = query[0].shape
    pairs = width // LANES
    by_pair = pl.BlockSpec((span, LANES), lambda i, at: (0, i))
    return pl.pallas_call(
        functools.partial(attend_kernel, group, count),
        grid_spec=pltpu.PrefetchScalarGridSpec(
            num_scalar_prefetch=1,
            grid=(pairs,),
            in_specs=[by_pair] * count
            + [pl.BlockSpec((1, span, 2 * LANES), lambda i, at: (i, 0, 0))] * 4,
            out_specs=[by_pair] * count
            + [pl.BlockSpec((1, 2, span), lambda i, at: (i, 0, 0))] * count,
            scratch_shapes=[
                pltpu.VMEM((count, 4, span, span), jnp.float32),
                pltpu.VMEM((2, 4, span, span), jnp.float32),
            ],
        ),
        out_shape=[jax.ShapeDtypeStruct((span, width), jnp.bfloat16)] * count
        + [jax.ShapeDtypeStruct((pairs, 2, span), jnp.float32)] * count,
        compiler_params=pltpu.CompilerParams(vmem_limit_bytes=VMEM_LIMIT),
        cost_estimate=pl.CostEstimate(
            flops=16 * count * span * 4 * span * width,
            bytes_accessed=2 * (2 * count + 8) * span * width,
            transcendentals=0,
        ),
    )(layout, *query, *keyval)


def attend_back_kernel(group, count, layout_ref, *refs):
    query = refs[:count]
    mixed = refs[count : 2 * count]
    grad = refs[2 * count : 3 * count]
    logsum = refs[3 * count : 4 * count]
    keyval = refs[4 * count : 4 * count + 4]
    query_grad = refs[4 * count + 4 : 5 * count + 4]
    near_ref, far_ref, bias_ref = refs[5 * count + 4 :]

    @pl.when(pl.program_id(0) == 0)
    def _():
        mask_into(bias_ref, layout_ref, group, count)

    turned_keys = [keyval[k][0, :, :LANES].T for k in range(4)]
    key_grads = [None] * 4
    value_grads = [None] * 4
    for q in range(count):
        weighed = (mixed[q][...].astype(jnp.float32) * grad[q][...].astype(jnp.float32)).T
        heads = []
        for h in range(2):
            chosen = one_head(query[q][...], h)
            chosen_grad = one_head(grad[q][...], h)
            delta = jnp.sum(weighed[h * HEAD : (h + 1) * HEAD, :], axis=0, keepdims=True)
            spread = logsum[q][0, h : h + 1, :]
            sums = None
            for k in range(4):
                scores = dot_nt(keyval[k][0, :, :LANES], chosen) + bias_ref[q, k]
                probs = jnp.exp(scores - spread)
                term = dot_nn(probs.astype(jnp.bfloat16), chosen_grad)
                value_grads[k] = term if value_grads[k] is None else value_grads[k] + term
                prob_grad = dot_nt(keyval[k][0, :, LANES:], chosen_grad)
                score_grad = (probs * (prob_grad - delta)).astype(jnp.bfloat16)
                term = dot_nn(score_grad, chosen)
                key_grads[k] = term if key_grads[k] is None else key_grads[k] + term
                term = dot_nn(turned_keys[k][h * HEAD : (h + 1) * HEAD, :], score_grad)
                sums = term if sums is None else sums + term
            heads.append(sums)
        query_grad[q][...] = jnp.concatenate(heads, axis=0).T * 0.125
    for k in range(4):
        ref = near_ref if k < 2 else far_ref
        ref[k % 2, 0, :, :LANES] = key_grads[k].astype(ref.dtype)
        ref[k % 2, 0, :, LANES:] = value_grads[k].astype(ref.dtype)


def attend_back(layout, query, mixed, grad, logsum, keyval, group):
    count = len(query)
    span, width = query[0].shape
    pairs = width // LANES
    by_pair = pl.BlockSpec((span, LANES), lambda i, at: (0, i))
    two_blocks = pl.BlockSpec((2, 1, span, 2 * LANES), lambda i, at: (0, i, 0, 0))
    return pl.pallas_call(
        functools.partial(attend_back_kernel, group, count),
        grid_spec=pltpu.PrefetchScalarGridSpec(
            num_scalar_prefetch=1,
            grid=(pairs,),
            in_specs=[by_pair] * (3 * count)
            + [pl.BlockSpec((1, 2, span), lambda i, at: (i, 0, 0))] * count
            + [pl.BlockSpec((1, span, 2 * LANES), lambda i, at: (i, 0, 0))] * 4,
            out_specs=[by_pair] * count + [two_blocks] * 2,
            scratch_shapes=[pltpu.VMEM((count, 4, span, span), jnp.float32)],
        ),
        out_shape=[jax.ShapeDtypeStruct((span, width), jnp.float32)] * count
        + [
            jax.ShapeDtypeStruct((2, pairs, span, 2 * LANES), jnp.float32),
            jax.ShapeDtypeStruct((2, pairs, span, 2 * LANES), jnp.bfloat16),
        ],
        compiler_params=pltpu.CompilerParams(vmem_limit_bytes=VMEM_LIMIT),
        cost_estimate=pl.CostEstimate(
            flops=40 * count * span * 4 * span * width,
            bytes_accessed=2 * (5 * count + 20) * span * width,
            transcendentals=0,
        ),
    )(layout, *query, *mixed, *grad, *logsum, *keyval)


def group_of(block):
    return 0 if block < 2 else 1


def feed_kernel(places_ref, *refs):
    mixed, hidden, cotan = refs[0:3], refs[3:6], refs[6:9]
    mod_ref, gain_ref, w_out_ref, w_one_ref, b_one_ref, w_two_ref, b_two_ref = refs[9:16]
    result, mixed_grad = refs[16:19], refs[19:22]
    resid_ref, low_ref, send_one, keep_one, send_two, keep_two, b_one_grad, sums_ref = refs[22:30]
    second_ref, turned_ref, branch_low_ref, branch_ref, second_grad_ref, act_ref, pre_ref = refs[30:]
    step = pl.program_id(0)
    span = hidden[0].shape[0]

    def modulation(block, which):
        return mod_ref[group_of(block), which : which + 1, :]

    @pl.when(step == 0)
    def _():
        bias_sum = None
        for b in range(3):
            rows = slice(b * span, (b + 1) * span)
            attended = dot_nn(mixed[b][...], w_out_ref[...])
            resid = hidden[b][...].astype(jnp.float32) + modulation(b, 2) * attended
            resid_ref[rows, :] = resid
            values, _ = normalized(resid)
            second = values * gain_ref[...] * (1.0 + modulation(b, 4)) + modulation(b, 3)
            second = second.astype(jnp.bfloat16)
            second_ref[rows, :] = second
            turned_ref[:, rows] = second.T
            branch_grad = modulation(b, 5) * cotan[b][...].astype(jnp.float32)
            branch_low_ref[rows, :] = branch_grad.astype(jnp.bfloat16)
            part = column_sum(branch_grad)
            bias_sum = part if bias_sum is None else bias_sum + part
        sums_ref[...] = jnp.zeros_like(sums_ref)
        sums_ref[1:2, :] = bias_sum
        branch_ref[...] = jnp.zeros_like(branch_ref)
        second_grad_ref[...] = jnp.zeros_like(second_grad_ref)

    b_one_grad[...] = jnp.zeros_like(b_one_grad)

    @pl.loop(0, 3)
    def _(b):
        rows = pl.ds(pl.multiple_of(b * span, span), span)
        pre = dot_nn(second_ref[rows, :], w_one_ref[...]) + b_one_ref[...]
        square = pre * pre
        tanh = jnp.tanh(GELU_A * pre * (1.0 + GELU_B * square))
        half = 0.5 * (1.0 + tanh)
        active = (pre * half).astype(jnp.bfloat16)
        act_ref[rows, :] = active
        branch_ref[rows, :] += dot_nn(active, w_two_ref[...])
        slope = half + 0.5 * GELU_A * pre * (1.0 - tanh * tanh) * (1.0 + 3.0 * GELU_B * square)
        pre_grad = dot_nt(branch_low_ref[rows, :], w_two_ref[...]) * slope
        b_one_grad[0] += column_sum(pre_grad)
        pre_low = pre_grad.astype(jnp.bfloat16)
        pre_ref[rows, :] = pre_low
        second_grad_ref[rows, :] += dot_nt(pre_low, w_one_ref[...])

    two_grad = dot_tn(act_ref[...], branch_low_ref[...]).astype(jnp.bfloat16)
    one_grad = dot_nn(turned_ref[...], pre_ref[...]).astype(jnp.bfloat16)

    @pl.when(step < 2)
    def _():
        send_two[0] = two_grad
        send_one[0] = one_grad

    @pl.when(step >= 2)
    def _():
        keep_two[0] = two_grad
        keep_one[0] = one_grad

    @pl.when(step == 3)
    def _():
        for b in range(3):
            at = 2 + 4 * group_of(b)
            rows = slice(b * span, (b + 1) * span)
            resid = resid_ref[rows, :]
            branch = branch_ref[rows, :] + b_two_ref[...]
            result[b][...] = (resid + modulation(b, 5) * branch).astype(jnp.bfloat16)
            upstream = cotan[b][...].astype(jnp.float32)
            sums_ref[at + 3 : at + 4, :] += column_sum(upstream * branch)
            values, inverse = normalized(resid)
            grad = second_grad_ref[rows, :]
            sums_ref[at + 1 : at + 2, :] += column_sum(grad)
            weighed = column_sum(grad * values)
            sums_ref[at + 2 : at + 3, :] += weighed * gain_ref[...]
            sums_ref[0:1, :] += weighed * (1.0 + modulation(b, 4))
            inner = grad * ((1.0 + modulation(b, 4)) * gain_ref[...])
            back = (inner - row_mean(inner) - values * row_mean(inner * values)) * inverse
            resid_grad = upstream + back
            resid_ref[rows, :] = resid_grad
            attended = dot_nn(mixed[b][...], w_out_ref[...])
            sums_ref[at : at + 1, :] += column_sum(resid_grad * attended)
            low = (modulation(b, 2) * resid_grad).astype(jnp.bfloat16)
            low_ref[rows, :] = low
            mixed_grad[b][...] = dot_nt(low, w_out_ref[...]).astype(jnp.bfloat16)


def feed(places, mixed, hidden, cotan, mod, gain, w_out, w_one, b_one, w_two, b_two):
    span, width = hidden[0].shape
    tokens = 3 * span
    once = pl.Buffered(1)
    block = pl.BlockSpec((span, width), lambda i, at: (0, 0), pipeline_mode=once)
    out_block = pl.BlockSpec((span, width), lambda i, at: (0, 0))
    every = pl.BlockSpec((tokens, width), lambda i, at: (0, 0))
    row = pl.BlockSpec((1, width), lambda i, at: (0, 0))
    send = pl.BlockSpec((1, width, width), lambda i, at: (jnp.minimum(i, 1), 0, 0))
    keep = pl.BlockSpec((1, width, width), lambda i, at: (jnp.maximum(i - 2, 0), 0, 0))
    low_block = jax.ShapeDtypeStruct((span, width), jnp.bfloat16)
    chunk_pair = jax.ShapeDtypeStruct((2, width, width), jnp.bfloat16)
    return pl.pallas_call(
        feed_kernel,
        grid_spec=pltpu.PrefetchScalarGridSpec(
            num_scalar_prefetch=1,
            grid=(4,),
            in_specs=[block] * 9
            + [
                pl.BlockSpec(mod.shape, lambda i, at: (0, 0, 0)),
                row,
                pl.BlockSpec((width, width), lambda i, at: (0, 0), pipeline_mode=once),
                pl.BlockSpec((width, width), lambda i, at: (0, chunk_at(i, at[0]))),
                pl.BlockSpec((1, width), lambda i, at: (0, chunk_at(i, at[0]))),
                pl.BlockSpec((width, width), lambda i, at: (chunk_at(i, at[0]), 0)),
                row,
            ],
            out_specs=[out_block] * 6
            + [every, every, send, keep, send, keep]
            + [
                pl.BlockSpec((1, 1, width), lambda i, at: (chunk_at(i, at[0]), 0, 0)),
                pl.BlockSpec((16, width), lambda i, at: (0, 0)),
            ],
            scratch_shapes=[
                pltpu.VMEM((tokens, width), jnp.bfloat16),
                pltpu.VMEM((width, tokens), jnp.bfloat16),
                pltpu.VMEM((tokens, width), jnp.bfloat16),
                pltpu.VMEM((tokens, width), jnp.float32),
                pltpu.VMEM((tokens, width), jnp.float32),
                pltpu.VMEM((tokens, width), jnp.bfloat16),
                pltpu.VMEM((tokens, width), jnp.bfloat16),
            ],
        ),
        out_shape=[low_block] * 6
        + [
            jax.ShapeDtypeStruct((tokens, width), jnp.float32),
            jax.ShapeDtypeStruct((tokens, width), jnp.bfloat16),
        ]
        + [chunk_pair] * 4
        + [
            jax.ShapeDtypeStruct((4, 1, width), jnp.float32),
            jax.ShapeDtypeStruct((16, width), jnp.float32),
        ],
        compiler_params=pltpu.CompilerParams(vmem_limit_bytes=VMEM_LIMIT),
        cost_estimate=pl.CostEstimate(
            flops=2 * tokens * 26 * width * width,
            bytes_accessed=2 * (14 * tokens * width + 17 * width * width),
            transcendentals=0,
        ),
    )(places, *mixed, *hidden, *cotan, mod, gain, w_out, w_one, b_one, w_two, b_two)


def merge_kernel(places_ref, *refs):
    query_grad = refs[0:3]
    near_own, got_own, near_split, got_split, got_chip = refs[3:8]
    angle, normed, mixed, hidden = refs[8:11], refs[11:14], refs[14:17], refs[17:20]
    low_ref, resid_grad_ref, mod_ref, gain_ref, weight_ref = refs[20:25]
    hidden_grad = refs[25:28]
    send_ref, keep_ref, sums_ref = refs[28:31]
    normed_ref, mixed_ref, grad_ref, total_ref = refs[31:]
    step = pl.program_id(0)
    chunk = chunk_at(step, places_ref[0])
    span = hidden[0].shape[0]
    pairs = hidden[0].shape[1] // LANES

    @pl.when(step == 0)
    def _():
        for b in range(3):
            rows = slice(b * span, (b + 1) * span)
            normed_ref[:, rows] = normed[b][...].T
            mixed_ref[:, rows] = mixed[b][...].T
        total_ref[...] = jnp.zeros_like(total_ref)

    def keyval_sum(block, pair, lanes):
        if block < 2:
            own, got = near_own, got_own
            at = block
        else:
            own, got = near_split, got_split
            at = 0
        total = own[at, pair, :, lanes] + got[at, pair, :, lanes].astype(jnp.float32)
        if block == 2:
            total = total + got_chip[pair, :, lanes].astype(jnp.float32)
        return total

    def put(result):
        @pl.when(step < 2)
        def _():
            send_ref[0] = result

        @pl.when(step >= 2)
        def _():
            keep_ref[0] = result

    @pl.when(chunk < 3)
    def _():
        for b in range(3):
            rows = slice(b * span, (b + 1) * span)
            for c in range(pairs):
                lanes = slice(c * LANES, (c + 1) * LANES)

                @pl.when(chunk == 0)
                def _(b=b, rows=rows, lanes=lanes):
                    (piece,) = turned(query_grad[b][:, lanes], angle[b][0], -angle[b][1])
                    grad_ref[rows, lanes] = piece.astype(jnp.bfloat16)

                @pl.when(chunk == 1)
                def _(b=b, c=c, rows=rows, lanes=lanes):
                    values = keyval_sum(b, c, slice(0, LANES))
                    (piece,) = turned(values, angle[b][0], -angle[b][1])
                    grad_ref[rows, lanes] = piece.astype(jnp.bfloat16)

                @pl.when(chunk == 2)
                def _(b=b, c=c, rows=rows, lanes=lanes):
                    values = keyval_sum(b, c, slice(LANES, 2 * LANES))
                    grad_ref[rows, lanes] = values.astype(jnp.bfloat16)

        put(dot_nn(normed_ref[...], grad_ref[...]).astype(jnp.bfloat16))
        total_ref[...] += dot_nt(grad_ref[...], weight_ref[...])

    @pl.when(chunk == 3)
    def _():
        put(dot_nn(mixed_ref[...], low_ref[...]).astype(jnp.bfloat16))

    @pl.when(step == 3)
    def _():
        sums_ref[...] = jnp.zeros_like(sums_ref)
        for b in range(3):
            group = group_of(b)
            at = 1 + 2 * group
            rows = slice(b * span, (b + 1) * span)
            values, inverse = normalized(hidden[b][...].astype(jnp.float32))
            grad = total_ref[rows, :]
            scaled = 1.0 + mod_ref[group, 1:2, :]
            weighed = column_sum(grad * values)
            sums_ref[0:1, :] += weighed * scaled
            sums_ref[at : at + 1, :] += column_sum(grad)
            sums_ref[at + 1 : at + 2, :] += weighed * gain_ref[...]
            inner = grad * (scaled * gain_ref[...])
            back = (inner - row_mean(inner) - values * row_mean(inner * values)) * inverse
            hidden_grad[b][...] = (resid_grad_ref[rows, :] + back).astype(jnp.bfloat16)


def merge_back(
    places, query_grad, keyval_grads, angle, normed, mixed, hidden, low, resid_grad, mod, gain, weight
):
    span, width = hidden[0].shape
    tokens = 3 * span
    once = pl.Buffered(1)

    def whole(array):
        return pl.BlockSpec(
            array.shape, lambda i, at: (0,) * len(array.shape), pipeline_mode=once
        )

    operands = [
        *query_grad, *keyval_grads, *angle, *normed, *mixed, *hidden, low, resid_grad, mod, gain
    ]
    return pl.pallas_call(
        merge_kernel,
        grid_spec=pltpu.PrefetchScalarGridSpec(
            num_scalar_prefetch=1,
            grid=(4,),
            in_specs=[whole(array) for array in operands]
            + [
                pl.BlockSpec(
                    (width, width), lambda i, at: (0, jnp.minimum(chunk_at(i, at[0]), 2))
                )
            ],
            out_specs=[pl.BlockSpec((span, width), lambda i, at: (0, 0))] * 3
            + [
                pl.BlockSpec((1, width, width), lambda i, at: (jnp.minimum(i, 1), 0, 0)),
                pl.BlockSpec((1, width, width), lambda i, at: (jnp.maximum(i - 2, 0), 0, 0)),
                pl.BlockSpec((8, width), lambda i, at: (0, 0)),
            ],
            scratch_shapes=[
                pltpu.VMEM((width, tokens), jnp.bfloat16),
                pltpu.VMEM((width, tokens), jnp.bfloat16),
                pltpu.VMEM((tokens, width), jnp.bfloat16),
                pltpu.VMEM((tokens, width), jnp.float32),
            ],
        ),
        out_shape=[jax.ShapeDtypeStruct((span, width), jnp.bfloat16)] * 3
        + [jax.ShapeDtypeStruct((2, width, width), jnp.bfloat16)] * 2
        + [jax.ShapeDtypeStruct((8, width), jnp.float32)],
        compiler_params=pltpu.CompilerParams(vmem_limit_bytes=VMEM_LIMIT),
        cost_estimate=pl.CostEstimate(
            flops=2 * tokens * 7 * width * width,
            bytes_accessed=2 * (18 * tokens * width + 7 * width * width),
            transcendentals=0,
        ),
    )(places, *operands, weight)


def swap(values, axis, bit):
    count = lax.axis_size(axis)
    return lax.ppermute(values, axis, [(i, i ^ bit) for i in range(count)])


def bit_of(axis, bit):
    return (lax.axis_index(axis) // bit) % 2


def batch_bits():
    count = lax.axis_size("batch")
    bits = []
    bit = 1
    while bit < count:
        bits.append(bit)
        bit *= 2
    return bits


def split_orders():
    bits = batch_bits()
    chip = ("seq", 2)
    split = [("batch", b) for b in bits[:3]]
    rest = [("batch", b) for b in bits[3:]]
    return ([chip] + split, split[:1] + [chip] + split[1:], rest)


def position_in(order):
    place = jnp.int32(0)
    for axis, bit in order:
        place = place * 2 + bit_of(axis, bit)
    return place


def total_of(parts):
    total = parts[0].astype(jnp.float32)
    for part in parts[1:]:
        total = total + part.astype(jnp.float32)
    return total.astype(jnp.bfloat16)


def scatter_group(first, second, order, rest):
    parts = [(first, 0), (second, 0)]
    rows = first.shape[0]
    for axis, bit in order:
        rows //= 2
        mine = bit_of(axis, bit)
        send = total_of(
            [lax.dynamic_slice_in_dim(p, at + (1 - mine) * rows, rows, 0) for p, at in parts]
        )
        parts = [(p, at + mine * rows) for p, at in parts] + [(swap(send, axis, bit), 0)]
    held = total_of([lax.dynamic_slice_in_dim(p, at, rows, 0) for p, at in parts])
    for axis, bit in rest:
        held = total_of([held, swap(held, axis, bit)])
    return held


def gather_group(held, order):
    blocks = held[None]
    for axis, bit in reversed(order):
        blocks = jnp.concatenate([blocks, swap(blocks, axis, bit)], axis=0)
    return blocks


def sync_piece(send, keep):
    order_a, order_b, rest = split_orders()
    got = swap(send, "seq", 1)
    out = []
    for g, order in ((0, order_a), (1, order_b)):
        held = scatter_group(keep[g], got[g], order, rest)
        full = gather_group(held, order)
        out.append((full, swap(full, "seq", 1)))
    (own_a, far_a), (own_b, far_b) = out
    return own_a, own_b, far_a, far_b


def place_scalars():
    order_a, order_b, _ = split_orders()
    return jnp.stack(
        [lax.axis_index("seq") % 2, position_in(order_a), position_in(order_b)]
    ).astype(jnp.int32)


def chunk_at(step, core):
    return jnp.where(step < 2, 2 * (1 - core) + step, 2 * core + step - 2)


def spread_blocks(places_ref, blocks_ref, group, out_ref):
    count, rows, _ = blocks_ref.shape
    for j in range(count):
        row = pl.multiple_of((places_ref[1 + group] ^ j) * rows, 16)
        out_ref[pl.ds(row, rows), :] = blocks_ref[j].astype(jnp.float32)


def finish_kernel(places_ref, own_a, own_b, far_a, far_b, out_ref):
    step = pl.program_id(0)
    for k, (ref, group) in enumerate(((own_a, 0), (own_b, 1), (far_a, 0), (far_b, 1))):

        @pl.when(step == k)
        def _(ref=ref, group=group):
            spread_blocks(places_ref, ref, group, out_ref)


def finish_two_kernel(places_ref, own_a, own_b, far_a, far_b, merged_ref, out_ref):
    step = pl.program_id(0)
    chunk = chunk_at(step, 1 - places_ref[0])
    for k, (ref, group) in enumerate(((own_a, 0), (own_b, 1), (far_a, 0), (far_b, 1))):

        @pl.when((step == k) & (chunk < 3))
        def _(ref=ref, group=group):
            spread_blocks(places_ref, ref, group, merged_ref)

        @pl.when((step == k) & (chunk == 3))
        def _(ref=ref, group=group):
            spread_blocks(places_ref, ref, group, out_ref)


def finish_piece(places, pieces, kind):
    count, rows, width = pieces[0].shape
    whole = pl.BlockSpec((count, rows, width), lambda i, at: (0, 0, 0))
    side = count * rows

    def own_first(i, at):
        return chunk_at(i, 1 - at[0])

    if kind == "rows":
        kernel = finish_kernel
        out_specs = pl.BlockSpec((side, width), lambda i, at: (own_first(i, at), 0))
        out_shape = jax.ShapeDtypeStruct((4 * side, width), jnp.float32)
    elif kind == "columns":
        kernel = finish_kernel
        out_specs = pl.BlockSpec((side, width), lambda i, at: (0, own_first(i, at)))
        out_shape = jax.ShapeDtypeStruct((side, 4 * width), jnp.float32)
    else:
        kernel = finish_two_kernel
        out_specs = [
            pl.BlockSpec((side, width), lambda i, at: (0, jnp.minimum(own_first(i, at), 2))),
            pl.BlockSpec((side, width), lambda i, at: (0, 0)),
        ]
        out_shape = [
            jax.ShapeDtypeStruct((side, 3 * width), jnp.float32),
            jax.ShapeDtypeStruct((side, width), jnp.float32),
        ]
    return pl.pallas_call(
        kernel,
        grid_spec=pltpu.PrefetchScalarGridSpec(
            num_scalar_prefetch=1, grid=(4,), in_specs=[whole] * 4, out_specs=out_specs
        ),
        out_shape=out_shape,
        compiler_params=pltpu.CompilerParams(vmem_limit_bytes=VMEM_LIMIT),
        cost_estimate=pl.CostEstimate(
            flops=0, bytes_accessed=6 * 4 * side * width, transcendentals=0
        ),
    )(places, *pieces)


def sum_small(vectors, mod_rows, cond):
    rows = vectors.shape[0]
    both = jnp.concatenate([vectors, mod_rows.reshape(-1, vectors.shape[1])], axis=0)
    for bit in (1, 2):
        both = both + swap(both, "seq", bit)
    vectors, own = both[:rows], both[rows:]
    everyone, conds = own, cond
    for bit in batch_bits():
        got = swap(jnp.concatenate([vectors, everyone], axis=0), "batch", bit)
        vectors = vectors + got[:rows]
        everyone = jnp.concatenate([everyone, got[rows:]], axis=0)
        conds = jnp.concatenate([conds, swap(conds, "batch", bit)], axis=0)
    return vectors, own.reshape(cond.shape[0], -1), everyone.reshape(conds.shape[0], -1), conds


def pick(values, index):
    return lax.dynamic_index_in_dim(values, index, 0, keepdims=False)


def rows_of(own, other, third, chip):
    first = jnp.where(chip == 0, own, other)
    second = jnp.where(chip == 0, other, own)
    return jnp.stack([first, second, third])


def shards(
    hidden,
    cond,
    lengths,
    ln1_gain,
    w_qkv,
    w_out,
    ln2_gain,
    w_fc1,
    b_fc1,
    w_fc2,
    b_fc2,
    w_ada,
    b_ada,
    cotangent,
):
    row_count, span, width = hidden.shape
    places = place_scalars()
    seat = lax.axis_index("seq")
    chip = seat // 2
    bases = jnp.stack([seat, seat ^ 2, seat ^ 1, seat ^ 3]) * span
    layout = jnp.concatenate(
        [pick(lengths, chip).reshape(-1), lengths[2], bases.astype(jnp.int32)]
    )
    hidden_far = swap(pick(hidden, 1 - chip), "seq", 2)
    blocks = [pick(hidden, chip), hidden_far, hidden[2]]
    ada_full = w_ada.astype(jnp.float32)
    modulation = (
        jnp.dot(cond, ada_full, precision=highest, preferred_element_type=jnp.float32) + b_ada
    )
    mod = jnp.stack([pick(modulation, chip), modulation[2]]).reshape(2, 6, width)
    gain_one, gain_two = ln1_gain[None], ln2_gain[None]

    normed_own, normed_split, query_own, query_split, kv_own, kv_split, angle_own, angle_split = (
        project(layout, [blocks[0], blocks[2]], mod, gain_one, w_qkv, (0, 1), (0, 0))
    )
    split_chip = swap(kv_split, "seq", 2)
    split_core = swap(kv_split, "seq", 1)
    split_cross = swap(split_chip, "seq", 1)
    own_core = swap(kv_own, "seq", 1)
    normed_far, query_far, kv_far, angle_far = project(
        layout, [blocks[1]], mod, gain_one, w_qkv, (0,), (1,)
    )
    far_core = swap(kv_far, "seq", 1)
    cotan_far = swap(pick(cotangent, 1 - chip), "seq", 2)
    cotan = [pick(cotangent, chip), cotan_far, cotangent[2]]
    kv_row = [kv_own, kv_far, own_core, far_core]
    kv_third = [kv_split, split_chip, split_core, split_cross]
    mixed_own, mixed_far, logsum_own, logsum_far = attend(
        layout, [query_own, query_far], kv_row, 0
    )
    mixed_split, logsum_split = attend(layout, [query_split], kv_third, 1)
    mixed = [mixed_own, mixed_far, mixed_split]
    (
        result_own,
        result_far,
        result_split,
        mixed_grad_own,
        mixed_grad_far,
        mixed_grad_split,
        resid_grad,
        low,
        send_one,
        keep_one,
        send_two,
        keep_two,
        b_one_grad,
        feed_sums,
    ) = feed(
        places,
        mixed,
        blocks,
        cotan,
        mod,
        gain_two,
        w_out,
        w_fc1,
        b_fc1[None],
        w_fc2,
        b_fc2[None],
    )
    fc2_pieces = sync_piece(send_two, keep_two)
    fc1_pieces = sync_piece(send_one, keep_one)
    output = rows_of(result_own, swap(result_far, "seq", 2), result_split, chip)

    query_grad_split, near_split, far_split = attend_back(
        layout, [query_split], [mixed_split], [mixed_grad_split], [logsum_split], kv_third, 1
    )
    got_split = swap(far_split, "seq", 1)
    chip_sum = (near_split[1] + got_split[1].astype(jnp.float32)).astype(jnp.bfloat16)
    got_chip = swap(chip_sum, "seq", 2)
    query_grad_own, query_grad_far, near_own, far_own = attend_back(
        layout,
        [query_own, query_far],
        [mixed_own, mixed_far],
        [mixed_grad_own, mixed_grad_far],
        [logsum_own, logsum_far],
        kv_row,
        0,
    )
    got_own = swap(far_own, "seq", 1)
    hidden_own_grad, hidden_far_grad, hidden_split_grad, send_att, keep_att, merge_sums = merge_back(
        places,
        [query_grad_own, query_grad_far, query_grad_split],
        [near_own, got_own, near_split, got_split, got_chip],
        [angle_own, angle_far, angle_split],
        [normed_own, normed_far, normed_split],
        mixed,
        blocks,
        low,
        resid_grad,
        mod,
        gain_one,
        w_qkv,
    )
    att_pieces = sync_piece(send_att, keep_att)
    hidden_grad = rows_of(hidden_own_grad, swap(hidden_far_grad, "seq", 2), hidden_split_grad, chip)

    vectors = jnp.concatenate(
        [merge_sums[0:1], feed_sums[0:1], feed_sums[1:2], b_one_grad.reshape(-1, width)], axis=0
    )

    def mod_row(group):
        at = 2 + 4 * group
        return jnp.concatenate(
            [
                merge_sums[1 + 2 * group : 3 + 2 * group],
                feed_sums[at : at + 4],
            ],
            axis=0,
        )

    row_own, row_split = mod_row(0), mod_row(1)
    nothing = jnp.zeros_like(row_own)
    mod_local = jnp.stack(
        [
            jnp.where(chip == 0, row_own, nothing),
            jnp.where(chip == 0, nothing, row_own),
            row_split,
        ]
    )
    vectors, mod_total, mod_all, cond_all = sum_small(vectors, mod_local, cond)
    ada_grad = jnp.dot(cond_all.T, mod_all, precision=highest, preferred_element_type=jnp.float32)
    cond_grad = jnp.dot(
        mod_total, ada_full.T, precision=highest, preferred_element_type=jnp.float32
    )
    qkv_grad, out_grad = finish_piece(places, att_pieces, "both")
    return (
        output,
        hidden_grad,
        cond_grad,
        vectors[0],
        qkv_grad,
        out_grad,
        vectors[1],
        finish_piece(places, fc1_pieces, "columns"),
        vectors[3:].reshape(-1),
        finish_piece(places, fc2_pieces, "rows"),
        vectors[2],
        ada_grad,
        jnp.sum(mod_all, axis=0),
    )


def solution(mesh):
    return jax.shard_map(
        shards,
        mesh=mesh,
        in_specs=(
            P("batch", "seq", None),
            P("batch", None),
            P("batch", None),
            P(),
            P(),
            P(),
            P(),
            P(),
            P(),
            P(),
            P(),
            P(),
            P(),
            P("batch", "seq", None),
        ),
        out_specs=(
            P("batch", "seq", None),
            P("batch", "seq", None),
            P("batch", None),
            P(),
            P(),
            P(),
            P(),
            P(),
            P(),
            P(),
            P(),
            P(),
            P(),
        ),
        check_vma=False,
    )
```

time: 716 us -> 518 us (0.72)
  Pallas kernels: 47.4 us -> 198 us
  local copies, waits for them, and re-layouts: 186 us -> 40.3 us
  matrix products: 139 us -> 6.58 us
  other arithmetic: 121 us -> 32.4 us
  waiting for transfers between devices: 124 us -> 171 us
  starting transfers between devices: 73 us -> 58.1 us
  between operations: 15.5 us -> 2.09 us
    pallas_call x3 -> x8, Pallas kernels: 25.9 us -> 176 us  [the longest x2 56.3 us: attend_back(): pl.pallas_call(functools.partial(attend_back_kernel, group, count), grid_...]
    dot_general x29 -> x0, matrix products: 131 us -> none  [the longest x3 33 us: attend_back(): jnp.einsum('chd,khd->hck', grad_heads, value_heads, preferred_element_typ...]
    ppermute x65 -> x77, waiting for transfers between devices: 72.9 us -> 171 us  [swap(): return lax.ppermute(values, axis, [(i, i ^ bit) for i in range(count)])]
    all_gather x2 -> x0, waiting for transfers between devices: 51.3 us -> none  [the longest x1 33.6 us: shards(): lax.all_gather(key_low, 'seq', axis=1, tiled=True)]
    dynamic_slice x30 -> x1, local copies, waits for them, and re-layouts: 42.7 us -> 0.04 us  [pick(): return lax.dynamic_index_in_dim(values, index, 0, keepdims=False)]
    concatenate x8 -> x2, local copies, waits for them, and re-layouts: 27.9 us -> 0.83 us  [mod_row(): jnp.concatenate([merge_sums[1 + 2 * group:3 + 2 * group], feed_sums[at:at...]
    dynamic_update_slice x15 -> x0, local copies, waits for them, and re-layouts: 25.1 us -> none  [the longest x9 20 us: shards(): lax.map(attend_back, (query_low, keys_all, values_all, mixed_grad, logsum...]
    reduce_sum x12 -> x0, other arithmetic: 24.7 us -> none  [the longest x3 10.9 us: attend(): total_sum = jnp.sum(expo, axis=-1, keepdims=True)]
  transfers between devices with their start and end apart: 69 -> 77, of which waited for: 23 -> 41; matrix products, arithmetic and copies ran while one was open for 26% -> 14% of each run, Pallas kernels for 6% -> 25%
where the time goes in v2:
time: 518 us; the launch traced here: 508 us
  Pallas kernels  198 us (38%)
  waiting for transfers between devices  171 us (33%)
  starting transfers between devices  58.1 us (11%)
  local copies, waits for them, and re-layouts  40.3 us (8%)
  other arithmetic  32.4 us (6%)
  matrix products  6.58 us (1%)
    ppermute x77, waiting for transfers between devices, swap(): return lax.ppermute(values, axis, [(i, i ^ bit) for i in range(count)])  171 us
    ppermute x77, starting transfers between devices, swap(): return lax.ppermute(values, axis, [(i, i ^ bit) for i in range(count)])  58.1 us
    pallas_call x2, Pallas kernels, attend_back(): pl.pallas_call(functools.partial(attend_back_kernel, group, count), grid_...  56.3 us
    pallas_call x1, Pallas kernels, feed(): pl.pallas_call(feed_kernel, grid_spec=pltpu.PrefetchScalarGridSpec(num_sc...  42.6 us
    pallas_call x2, Pallas kernels, attend(): pl.pallas_call(functools.partial(attend_kernel, group, count), grid_spec=...  29.8 us
    pallas_call x1, Pallas kernels, merge_back(): pl.pallas_call(merge_kernel, grid_spec=pltpu.PrefetchScalarGridSpec(num_s...  28.6 us
    pallas_call x3, Pallas kernels, finish_piece(): pl.pallas_call(kernel, grid_spec=pltpu.PrefetchScalarGridSpec(num_scalar_...  21.7 us
    pallas_call x2, Pallas kernels, project(): pl.pallas_call(functools.partial(project_kernel, groups, bases), grid_spe...  18.5 us
  transfers between devices with their start and end apart: 77, of which 41 were waited for; matrix products, arithmetic and copies ran while one was open for 14% of the time, Pallas kernels for 25%

profile of v2, /device:TPU:0, one launch (start us, length us, event | category | flops | bytes accessed | tf_op | source)
XLA Modules:
  0.0 508.1 jit_solution(3650214215310206236)
XLA Ops:
  9.2 11.4 %shard_map.237 = (bf16[256,768]{1,0:T(8,128)(2,1)}, bf16[256,768]{1,0:T(8,128)(2,1)}, bf16[256,768]{1,0:T(8,128)(2,1)}, bf16[256,768]{1,0:T(8,128)(2,1)}, bf16[6...) custom-call(s32[20]{0:T(128)} %pad_add_fusion.1.layout_ref, ...), custom_call_target="tpu_custom_call" | custom-call | flops 1811939328 | bytes 7471104 | tf_op jit(solution)/shard_map/pallas_call | solution.py:141
  21.4 7.1 %shard_map.238 = (bf16[256,768]{1,0:T(8,128)(2,1)}, bf16[256,768]{1,0:T(8,128)(2,1)}, bf16[6,256,256]{2,1,0:T(8,128)(2,1)}, f32[2,256,128]{2,1,0:T(8,128)}) custom-call(s32[20]{0:T(128)} %pad_add_fusion.1.layout_ref, bf16[256,768]{1,0:T(8,128)(2,1)} %copy-done.16, f32[2,6,768]{2,1,0:T(8,128)} %reshape.268.refs_2_.refs_1_.refs_9_.refs_22_, ...), custom_call_target="tpu_custom_call" | custom-call | flops 905969664 | bytes 5505024 | tf_op jit(solution)/shard_map/pallas_call | solution.py:141
  29.2 10.7 %collective-permute-done.3.refs_2_.refs_5_ = bf16[6,256,256]{2,1,0:T(8,128)(2,1)} collective-permute-done((bf16[6,256,256]{2,1,0:T(8,128)(2,1)}, bf16[6,256,256]{2,1,0:T(8,128)(2,1)}, u32[]{:S(2)}, u32[]{:S(2)}) %collective-permute-start.3) | collective-permute-done | bytes 786464 | tf_op jit(solution)/shard_map/ppermute | solution.py:629
  43.9 18.1 %shard_map.239 = (bf16[256,768]{1,0:T(8,128)(2,1)}, bf16[256,768]{1,0:T(8,128)(2,1)}, f32[6,2,256]{2,1,0:T(2,128)}, f32[6,2,256]{2,1,0:T(2,128)}) custom-call(s32[20]{0:T(128)} %pad_add_fusion.1.layout_ref, bf16[256,768]{1,0:T(8,128)(2,1)} %get-tuple-element.60.refs_0_, bf16[256,768]{1,0:T(8,128)(2,1)} %get-tuple-element.61.refs_1_, ...), custom_call_target="tpu_custom_call" | custom-call | flops 6442450944 | bytes 4718592 | tf_op jit(solution)/shard_map/pallas_call | solution.py:226
  62.0 11.7 %shard_map.240 = (bf16[256,768]{1,0:T(8,128)(2,1)}, f32[6,2,256]{2,1,0:T(2,128)}) custom-call(s32[20]{0:T(128)} %pad_add_fusion.1.layout_ref, bf16[256,768]{1,0:T(8,128)(2,1)} %get-tuple-element.66.refs_0_, bf16[6,256,256]{2,1,0:T(8,128)(2,1)} %get-tuple-element.67.refs_1_.refs_4_, bf16[6,256,256]{2,1,0:T(8,128)(2,1)} %collective-permute-done.3.refs_2_.refs_5_, ...), custom_call_target="tpu_custom_call" | custom-call | flops 3221225472 | bytes 3932160 | tf_op jit(solution)/shard_map/pallas_call | solution.py:226
  74.5 42.6 %shard_map.241 = (bf16[256,768]{1,0:T(8,128)(2,1)}, bf16[256,768]{1,0:T(8,128)(2,1)}, bf16[256,768]{1,0:T(8,128)(2,1)}, bf16[256,768]{1,0:T(8,128)(2,1)}, bf16[2...) custom-call(s32[3]{0:T(128)} %pad_add_fusion.places_ref, ...), custom_call_target="tpu_custom_call" | custom-call | flops 23555211264 | bytes 36569088 | tf_op jit(solution)/shard_map/pallas_call | solution.py:435
  117.1 17.8 %shard_map.243 = (f32[256,768]{1,0:T(8,128)}, f32[2,6,256,256]{3,2,1,0:T(8,128)}, bf16[2,6,256,256]{3,2,1,0:T(8,128)(2,1)}) custom-call(s32[20]{0:T(128)} %pad_add_fusion.1.layout_ref, bf16[256,768]{1,0:T(8,128)(2,1)} %get-tuple-element.66.refs_0_, bf16[256,768]{1,0:T(8,128)(2,1)} %get-tuple-element.68.refs_2_.refs_1_.refs_16_, ...), custom_call_target="tpu_custom_call" | custom-call | flops 8053063680 | bytes 9830400 | tf_op jit(solution)/shard_map/pallas_call | solution.py:301
  135.2 38.5 %shard_map.242 = (f32[256,768]{1,0:T(8,128)}, f32[256,768]{1,0:T(8,128)}, f32[2,6,256,256]{3,2,1,0:T(8,128)}, bf16[2,6,256,256]{3,2,1,0:T(8,128)(2,1)}) custom-call(s32[20]{0:T(128)} %pad_add_fusion.1.layout_ref, bf16[256,768]{1,0:T(8,128)(2,1)} %get-tuple-element.60.refs_0_, bf16[256,768]{1,0:T(8,128)(2,1)} %get-tuple-element.61.refs_1_, ...), custom_call_target="tpu_custom_call" | custom-call | flops 16106127360 | bytes 11796480 | tf_op jit(solution)/shard_map/pallas_call | solution.py:301
  196.2 14.4 %collective-permute-done.10.refs_7_ = bf16[6,256,256]{2,1,0:T(8,128)(2,1)} collective-permute-done((bf16[6,256,256]{2,1,0:T(8,128)(2,1)S(1)}, bf16[6,256,256]{2,1,0:T(8,128)(2,1)}, u32[]{:S(2)}, u32[]{:S(2)}) %collective-permute-start.10) | collective-permute-done | bytes 786464 | tf_op jit(solution)/shard_map/ppermute | solution.py:629
  210.5 28.6 %shard_map.244 = (bf16[256,768]{1,0:T(8,128)(2,1)}, bf16[256,768]{1,0:T(8,128)(2,1)}, bf16[256,768]{1,0:T(8,128)(2,1)}, bf16[2,768,768]{2,1,0:T(8,128)(2,1)}, bf...) custom-call(s32[3]{0:T(128)} %pad_add_fusion.places_ref, f32[256,768]{1,0:T(8,128)} %get-tuple-element.76.refs_0_, ...), custom_call_target="tpu_custom_call" | custom-call | flops 6341787648 | bytes 29491200 | tf_op jit(solution)/shard_map/pallas_call | solution.py:591
  255.4 13.3 %collective-permute-done.13 = f32[25,768]{1,0:T(8,128)S(1)} collective-permute-done((f32[25,768]{1,0:T(8,128)S(1)}, f32[25,768]{1,0:T(8,128)S(1)}, u32[]{:S(2)}, u32[]{:S(2)}) %collective-permute-start.13) | collective-permute-done | bytes 76832 | tf_op jit(solution)/shard_map/ppermute | solution.py:629
  354.0 5.2 %collective-permute-done.43 = bf16[4,48,768]{2,1,0:T(8,128)(2,1)S(1)} collective-permute-done((bf16[4,48,768]{2,1,0:T(8,128)(2,1)S(1)}, bf16[4,48,768]{2,1,0:T(8,128)(2,1)S(1)}, u32[]{:S(2)}, u32[]{:S(2)}) %collective-permute-start.43) | collective-permute-done | bytes 294944 | tf_op jit(solution)/shard_map/ppermute | solution.py:629
  370.2 21.4 %collective-permute-done.18 = bf16[384,768]{1,0:T(8,128)(2,1)S(1)} collective-permute-done((bf16[384,768]{1,0:T(8,128)(2,1)S(1)}, bf16[384,768]{1,0:T(8,128)(2,1)S(1)}, u32[]{:S(2)}, u32[]{:S(2)}) %collective-permute-start.18) | collective-permute-done | bytes 589856 | tf_op jit(solution)/shard_map/ppermute | solution.py:629
  395.6 6.1 %collective-permute-done.19 = bf16[192,768]{1,0:T(8,128)(2,1)S(1)} collective-permute-done((bf16[192,768]{1,0:T(8,128)(2,1)S(1)}, bf16[192,768]{1,0:T(8,128)(2,1)S(1)}, u32[]{:S(2)}, u32[]{:S(2)}) %collective-permute-start.19) | collective-permute-done | bytes 294944 | tf_op jit(solution)/shard_map/ppermute | solution.py:629
  402.0 9.4 %collective-permute-done.27 = bf16[192,768]{1,0:T(8,128)(2,1)S(1)} collective-permute-done((bf16[192,768]{1,0:T(8,128)(2,1)S(1)}, bf16[192,768]{1,0:T(8,128)(2,1)S(1)}, u32[]{:S(2)}, u32[]{:S(2)}) %collective-permute-start.27) | collective-permute-done | bytes 294944 | tf_op jit(solution)/shard_map/ppermute | solution.py:629
  418.3 6.0 %collective-permute-done.21 = bf16[48,768]{1,0:T(8,128)(2,1)S(1)} collective-permute-done((bf16[48,768]{1,0:T(8,128)(2,1)S(1)}, bf16[48,768]{1,0:T(8,128)(2,1)S(1)}, u32[]{:S(2)}, u32[]{:S(2)}) %collective-permute-start.21) | collective-permute-done | bytes 73760 | tf_op jit(solution)/shard_map/ppermute | solution.py:629
  424.3 6.9 %collective-permute-done.29 = bf16[48,768]{1,0:T(8,128)(2,1)S(1)} collective-permute-done((bf16[48,768]{1,0:T(8,128)(2,1)S(1)}, bf16[48,768]{1,0:T(8,128)(2,1)S(1)}, u32[]{:S(2)}, u32[]{:S(2)}) %collective-permute-start.29) | collective-permute-done | bytes 73760 | tf_op jit(solution)/shard_map/ppermute | solution.py:629
  436.7 5.1 %collective-permute-done.30 = bf16[1,48,768]{2,1,0:T(8,128)(2,1)S(1)} collective-permute-done((bf16[1,48,768]{2,1,0:T(8,128)(2,1)S(1)}, bf16[1,48,768]{2,1,0:T(8,128)(2,1)S(1)}, u32[]{:S(2)}, u32[]{:S(2)}) %collective-permute-start.30) | collective-permute-done | bytes 73760 | tf_op jit(solution)/shard_map/ppermute | solution.py:629
  450.5 6.4 %collective-permute-done.24 = bf16[4,48,768]{2,1,0:T(8,128)(2,1)S(1)} collective-permute-done((bf16[4,48,768]{2,1,0:T(8,128)(2,1)S(1)}, bf16[4,48,768]{2,1,0:T(8,128)(2,1)S(1)}, u32[]{:S(2)}, u32[]{:S(2)}) %collective-permute-start.24) | collective-permute-done | bytes 294944 | tf_op jit(solution)/shard_map/ppermute | solution.py:629
  461.2 5.7 %collective-permute-done.25 = bf16[8,48,768]{2,1,0:T(8,128)(2,1)S(1)} collective-permute-done((bf16[8,48,768]{2,1,0:T(8,128)(2,1)S(1)}, bf16[8,48,768]{2,1,0:T(8,128)(2,1)S(1)}, u32[]{:S(2)}, u32[]{:S(2)}) %collective-permute-start.25) | collective-permute-done | bytes 589856 | tf_op jit(solution)/shard_map/ppermute | solution.py:629
  469.5 6.5 %collective-permute-done.16 = f32[79,768]{1,0:T(8,128)S(1)} collective-permute-done((f32[79,768]{1,0:T(8,128)S(1)}, f32[79,768]{1,0:T(8,128)S(1)}, u32[]{:S(2)}, u32[]{:S(2)}) %collective-permute-start.16) | collective-permute-done | bytes 242720 | tf_op jit(solution)/shard_map/ppermute | solution.py:629
  485.9 7.0 %shard_map.246 = f32[768,3072]{1,0:T(8,128)} custom-call(s32[3]{0:T(128)} %pad_add_fusion.places_ref, bf16[16,48,768]{2,1,0:T(8,128)(2,1)} %copy-done.18, bf16[16,48,768]{2,1,0:T(8,128)(2,1)} %constant_dynamic-update-slice_fusion.15.own_b, bf16[16,48,768]{2,1,0:T(8,128)(2,1)} %copy-done.22, bf16[16,48,768]{2,1,0:T(8,128)(2,1)} %collective-permute-done.54.far_b), custom_call_target="tpu_custom_call" | custom-call | bytes 14155776 | tf_op jit(solution)/shard_map/pallas_call | solution.py:770
  492.9 7.0 %shard_map.247 = f32[3072,768]{1,0:T(8,128)} custom-call(s32[3]{0:T(128)} %pad_add_fusion.places_ref, bf16[16,48,768]{2,1,0:T(8,128)(2,1)} %constant_dynamic-update-slice_fusion.20.own_a, bf16[16,48,768]{2,1,0:T(8,128)(2,1)} %constant_dynamic-update-slice_fusion.25.own_b, bf16[16,48,768]{2,1,0:T(8,128)(2,1)} %collective-permute-done.72.far_a, ...), custom_call_target="tpu_custom_call" | custom-call | bytes 14155776 | tf_op jit(solution)/shard_map/pallas_call | solution.py:770
  499.9 7.8 %shard_map.245 = (f32[768,2304]{1,0:T(8,128)}, f32[768,768]{1,0:T(8,128)}) custom-call(s32[3]{0:T(128)} %pad_add_fusion.places_ref, bf16[16,48,768]{2,1,0:T(8,128)(2,1)} %copy-done.17, bf16[16,48,768]{2,1,0:T(8,128)(2,1)} %constant_dynamic-update-slice_fusion.5.own_b, bf16[16,48,768]{2,1,0:T(8,128)(2,1)} %collective-permute-done.34.far_a, ...), custom_call_target="tpu_custom_call" | custom-call | bytes 14155776 | tf_op jit(solution)/shard_map/pallas_call | solution.py:770
  (369 shorter events, 191.4 us)
Async XLA Ops:
  20.6 22.3 %collective-permute-start.1 = (bf16[6,256,256]{2,1,0:T(8,128)(2,1)}, bf16[6,256,256]{2,1,0:T(8,128)(2,1)}, u32[]{:S(2)}, u32[]{:S(2)}) collective-permute-start(bf16[6,256,256]{2,1,0:T(8,128)(2,1)} %get-tuple-element.62.refs_2_.refs_8_), channel_id=1, source_target_pairs={{0,8},{8,0},{16,24},{24,16},{1,9},{9,1},{17,25},{25,17},{2,10},{10... | collective-permute-start | bytes 2359304 | tf_op jit(solution)/shard_map/ppermute | solution.py:629
  29.1 32.9 %collective-permute-start.4 = (bf16[6,256,256]{2,1,0:T(8,128)(2,1)}, bf16[6,256,256]{2,1,0:T(8,128)(2,1)}, u32[]{:S(2)}, u32[]{:S(2)}) collective-permute-start(bf16[6,256,256]{2,1,0:T(8,128)(2,1)} %get-tuple-element.67.refs_1_.refs_4_), channel_id=1, source_target_pairs={{0,8},{8,0},{16,24},{24,16},{1,9},{9,1},{17,25},{25,17},{2,10},{10... | collective-permute-start | bytes 2359304 | tf_op jit(solution)/shard_map/ppermute | solution.py:629
  39.9 22.1 %collective-permute-start.5 = (bf16[6,256,256]{2,1,0:T(8,128)(2,1)}, bf16[6,256,256]{2,1,0:T(8,128)(2,1)}, u32[]{:S(2)}, u32[]{:S(2)}) collective-permute-start(bf16[6,256,256]{2,1,0:T(8,128)(2,1)} %collective-permute-done.3.refs_2_.refs_5_), channel_id=1, source_target_pairs={{0,8},{8,0},{16,24},{24,16},{1,9},{9,1},{17,25},{25,17},{2,10},{10... | collective-permute-start | bytes 2359304 | tf_op jit(solution)/shard_map/ppermute | solution.py:629
  40.8 32.9 %collective-permute-start.6 = (bf16[256,768]{1,0:T(8,128)(2,1)S(1)}, bf16[256,768]{1,0:T(8,128)(2,1)S(1)}, u32[]{:S(2)}, u32[]{:S(2)}) collective-permute-start(bf16[256,768]{1,0:T(8,128)(2,1)S(1)} %get-tuple-element.136), channel_id=1, source_target_pairs={{0,16},{8,24},{16,0},{24,8},{1,17},{9,25},{17,1},{25,9},{2,18},{10... | collective-permute-start | bytes 1179656 | tf_op jit(solution)/shard_map/ppermute | solution.py:629
  134.9 51.9 %collective-permute-start.9 = (bf16[2,6,256,256]{3,2,1,0:T(8,128)(2,1)}, bf16[2,6,256,256]{3,2,1,0:T(8,128)(2,1)S(1)}, u32[]{:S(2)}, u32[]{:S(2)}) collective-permute-start(bf16[2,6,256,256]{3,2,1,0:T(8,128)(2,1)} %get-tuple-element.84), channel_id=1, source_target_pairs={{0,8},{8,0},{16,24},{24,16},{1,9},{9,1},{17,25},{25,17},{2,10},{10... | collective-permute-start | bytes 4718600 | tf_op jit(solution)/shard_map/ppermute | solution.py:629
  173.6 22.5 %collective-permute-start.8 = (bf16[2,6,256,256]{3,2,1,0:T(8,128)(2,1)}, bf16[2,6,256,256]{3,2,1,0:T(8,128)(2,1)}, u32[]{:S(2)}, u32[]{:S(2)}) collective-permute-start(bf16[2,6,256,256]{3,2,1,0:T(8,128)(2,1)} %get-tuple-element.82), channel_id=1, source_target_pairs={{0,8},{8,0},{16,24},{24,16},{1,9},{9,1},{17,25},{25,17},{2,10},{10... | collective-permute-start | bytes 4718600 | tf_op jit(solution)/shard_map/ppermute | solution.py:629
  181.9 287.0 %collective-permute-start.76 = (f32[12,128]{1,0:T(8,128)}, f32[12,128]{1,0:T(8,128)}, u32[]{:S(2)}, u32[]{:S(2)}) collective-permute-start(f32[12,128]{1,0:T(8,128)} %pad_maximum_fusion.27), channel_id=1, source_target_pairs={{0,4},{1,5},{2,6},{3,7},{4,0},{5,1},{6,2},{7,3},{8,12},{9,13},{10,... | collective-permute-start | bytes 18440 | tf_op jit(solution)/shard_map/ppermute | solution.py:629
  186.8 60.8 %collective-permute-start.36 = (bf16[2,768,768]{2,1,0:T(8,128)(2,1)}, bf16[2,768,768]{2,1,0:T(8,128)(2,1)}, u32[]{:S(2)}, u32[]{:S(2)}) collective-permute-start(bf16[2,768,768]{2,1,0:T(8,128)(2,1)} %get-tuple-element.104), channel_id=1, source_target_pairs={{0,8},{8,0},{16,24},{24,16},{1,9},{9,1},{17,25},{25,17},{2,10},{10... | collective-permute-start | bytes 7077896 | tf_op jit(solution)/shard_map/ppermute | solution.py:629
  189.1 21.4 %collective-permute-start.10 = (bf16[6,256,256]{2,1,0:T(8,128)(2,1)S(1)}, bf16[6,256,256]{2,1,0:T(8,128)(2,1)}, u32[]{:S(2)}, u32[]{:S(2)}) collective-permute-start(bf16[6,256,256]{2,1,0:T(8,128)(2,1)S(1)} %fusion), channel_id=1, source_target_pairs={{0,16},{8,24},{16,0},{24,8},{1,17},{9,25},{17,1},{25,9},{2,18},{10... | collective-permute-start | bytes 2359304 | tf_op jit(solution)/shard_map/ppermute | solution.py:629
  194.9 75.4 %collective-permute-start.55 = (bf16[2,768,768]{2,1,0:T(8,128)(2,1)}, bf16[2,768,768]{2,1,0:T(8,128)(2,1)}, u32[]{:S(2)}, u32[]{:S(2)}) collective-permute-start(bf16[2,768,768]{2,1,0:T(8,128)(2,1)} %get-tuple-element.106), channel_id=1, source_target_pairs={{0,8},{8,0},{16,24},{24,16},{1,9},{9,1},{17,25},{25,17},{2,10},{10... | collective-permute-start | bytes 7077896 | tf_op jit(solution)/shard_map/ppermute | solution.py:629
  250.7 34.3 %collective-permute-start.37 = (bf16[384,768]{1,0:T(8,128)(2,1)}, bf16[384,768]{1,0:T(8,128)(2,1)}, u32[]{:S(2)}, u32[]{:S(2)}) collective-permute-start(bf16[384,768]{1,0:T(8,128)(2,1)} %fusion.3), channel_id=1, source_target_pairs={{0,16},{8,24},{16,0},{24,8},{1,17},{9,25},{17,1},{25,9},{2,18},{10... | collective-permute-start | bytes 1769480 | tf_op jit(solution)/shard_map/ppermute | solution.py:629
  253.9 32.5 %collective-permute-start.45 = (bf16[384,768]{1,0:T(8,128)(2,1)}, bf16[384,768]{1,0:T(8,128)(2,1)}, u32[]{:S(2)}, u32[]{:S(2)}) collective-permute-start(bf16[384,768]{1,0:T(8,128)(2,1)} %fusion.4), channel_id=1, source_target_pairs={{0,1},{1,0},{2,3},{3,2},{4,5},{5,4},{6,7},{7,6},{8,9},{9,8},{10,11... | collective-permute-start | bytes 1769480 | tf_op jit(solution)/shard_map/ppermute | solution.py:629
  285.0 77.4 %collective-permute-start.17 = (bf16[2,768,768]{2,1,0:T(8,128)(2,1)}, bf16[2,768,768]{2,1,0:T(8,128)(2,1)S(1)}, u32[]{:S(2)}, u32[]{:S(2)}) collective-permute-start(bf16[2,768,768]{2,1,0:T(8,128)(2,1)} %get-tuple-element.100), channel_id=1, source_target_pairs={{0,8},{8,0},{16,24},{24,16},{1,9},{9,1},{17,25},{25,17},{2,10},{10... | collective-permute-start | bytes 7077896 | tf_op jit(solution)/shard_map/ppermute | solution.py:629
  361.5 30.8 %collective-permute-start.44 = (bf16[8,48,768]{2,1,0:T(8,128)(2,1)S(1)}, bf16[8,48,768]{2,1,0:T(8,128)(2,1)S(1)}, u32[]{:S(2)}, u32[]{:S(2)}) collective-permute-start(bf16[8,48,768]{2,1,0:T(8,128)(2,1)S(1)} %pad_maximum_fusion.4), channel_id=1, source_target_pairs={{0,16},{8,24},{16,0},{24,8},{1,17},{9,25},{17,1},{25,9},{2,18},{10... | collective-permute-start | bytes 1769480 | tf_op jit(solution)/shard_map/ppermute | solution.py:629
  363.8 27.8 %collective-permute-start.18 = (bf16[384,768]{1,0:T(8,128)(2,1)S(1)}, bf16[384,768]{1,0:T(8,128)(2,1)S(1)}, u32[]{:S(2)}, u32[]{:S(2)}) collective-permute-start(bf16[384,768]{1,0:T(8,128)(2,1)S(1)} %fusion.1), channel_id=1, source_target_pairs={{0,16},{8,24},{16,0},{24,8},{1,17},{9,25},{17,1},{25,9},{2,18},{10... | collective-permute-start | bytes 1769480 | tf_op jit(solution)/shard_map/ppermute | solution.py:629
  365.3 26.5 %collective-permute-start.26 = (bf16[384,768]{1,0:T(8,128)(2,1)S(1)}, bf16[384,768]{1,0:T(8,128)(2,1)S(1)}, u32[]{:S(2)}, u32[]{:S(2)}) collective-permute-start(bf16[384,768]{1,0:T(8,128)(2,1)S(1)} %fusion.2), channel_id=1, source_target_pairs={{0,1},{1,0},{2,3},{3,2},{4,5},{5,4},{6,7},{7,6},{8,9},{9,8},{10,11... | collective-permute-start | bytes 1769480 | tf_op jit(solution)/shard_map/ppermute | solution.py:629
  369.1 25.3 %collective-permute-start.52 = (bf16[8,48,768]{2,1,0:T(8,128)(2,1)S(1)}, bf16[8,48,768]{2,1,0:T(8,128)(2,1)S(1)}, u32[]{:S(2)}, u32[]{:S(2)}) collective-permute-start(bf16[8,48,768]{2,1,0:T(8,128)(2,1)S(1)} %pad_maximum_fusion.5), channel_id=1, source_target_pairs={{0,1},{1,0},{2,3},{3,2},{4,5},{5,4},{6,7},{7,6},{8,9},{9,8},{10,11... | collective-permute-start | bytes 1769480 | tf_op jit(solution)/shard_map/ppermute | solution.py:629
  394.4 75.0 %collective-permute-start.11 = (bf16[256,768]{1,0:T(8,128)(2,1)S(1)}, bf16[256,768]{1,0:T(8,128)(2,1)S(1)}, u32[]{:S(2)}, u32[]{:S(2)}) collective-permute-start(bf16[256,768]{1,0:T(8,128)(2,1)S(1)} %copy-done.47), channel_id=1, source_target_pairs={{0,16},{8,24},{16,0},{24,8},{1,17},{9,25},{17,1},{25,9},{2,18},{10... | collective-permute-start | bytes 1179656 | tf_op jit(solution)/shard_map/ppermute | solution.py:629
  401.7 40.1 %collective-permute-start.71 = (bf16[8,48,768]{2,1,0:T(8,128)(2,1)S(1)}, bf16[8,48,768]{2,1,0:T(8,128)(2,1)S(1)}, u32[]{:S(2)}, u32[]{:S(2)}) collective-permute-start(bf16[8,48,768]{2,1,0:T(8,128)(2,1)S(1)} %pad_maximum_fusion.7), channel_id=1, source_target_pairs={{0,1},{1,0},{2,3},{3,2},{4,5},{5,4},{6,7},{7,6},{8,9},{9,8},{10,11... | collective-permute-start | bytes 1769480 | tf_op jit(solution)/shard_map/ppermute | solution.py:629
  416.6 59.3 %collective-permute-start.53 = (bf16[16,48,768]{2,1,0:T(8,128)(2,1)S(1)}, bf16[16,48,768]{2,1,0:T(8,128)(2,1)S(1)}, u32[]{:S(2)}, u32[]{:S(2)}) collective-permute-start(bf16[16,48,768]{2,1,0:T(8,128)(2,1)S(1)} %constant_dynamic-update-slice_fusion.10.own_a), channel_id=1, source_target_pairs={{0,8},{8,0},{16,24},{24,16},{1,9},{9,1},{17,25},{25,17},{2,10},{10... | collective-permute-start | bytes 3538952 | tf_op jit(solution)/shard_map/ppermute | solution.py:629
  468.9 24.0 %collective-permute-start.72 = (bf16[16,48,768]{2,1,0:T(8,128)(2,1)}, bf16[16,48,768]{2,1,0:T(8,128)(2,1)}, u32[]{:S(2)}, u32[]{:S(2)}) collective-permute-start(bf16[16,48,768]{2,1,0:T(8,128)(2,1)} %constant_dynamic-update-slice_fusion.20.own_a), channel_id=1, source_target_pairs={{0,8},{8,0},{16,24},{24,16},{1,9},{9,1},{17,25},{25,17},{2,10},{10... | collective-permute-start | bytes 3538952 | tf_op jit(solution)/shard_map/ppermute | solution.py:629
  469.4 23.5 %collective-permute-start.73 = (bf16[16,48,768]{2,1,0:T(8,128)(2,1)}, bf16[16,48,768]{2,1,0:T(8,128)(2,1)}, u32[]{:S(2)}, u32[]{:S(2)}) collective-permute-start(bf16[16,48,768]{2,1,0:T(8,128)(2,1)} %constant_dynamic-update-slice_fusion.25.own_b), channel_id=1, source_target_pairs={{0,8},{8,0},{16,24},{24,16},{1,9},{9,1},{17,25},{25,17},{2,10},{10... | collective-permute-start | bytes 3538952 | tf_op jit(solution)/shard_map/ppermute | solution.py:629
  476.0 23.9 %collective-permute-start.34 = (bf16[16,48,768]{2,1,0:T(8,128)(2,1)S(1)}, bf16[16,48,768]{2,1,0:T(8,128)(2,1)}, u32[]{:S(2)}, u32[]{:S(2)}) collective-permute-start(bf16[16,48,768]{2,1,0:T(8,128)(2,1)S(1)} %constant_dynamic-update-slice_fusion.own_a), channel_id=1, source_target_pairs={{0,8},{8,0},{16,24},{24,16},{1,9},{9,1},{17,25},{25,17},{2,10},{10... | collective-permute-start | bytes 3538952 | tf_op jit(solution)/shard_map/ppermute | solution.py:629
  476.0 23.9 %collective-permute-start.35 = (bf16[16,48,768]{2,1,0:T(8,128)(2,1)}, bf16[16,48,768]{2,1,0:T(8,128)(2,1)}, u32[]{:S(2)}, u32[]{:S(2)}) collective-permute-start(bf16[16,48,768]{2,1,0:T(8,128)(2,1)} %constant_dynamic-update-slice_fusion.5.own_b), channel_id=1, source_target_pairs={{0,8},{8,0},{16,24},{24,16},{1,9},{9,1},{17,25},{25,17},{2,10},{10... | collective-permute-start | bytes 3538952 | tf_op jit(solution)/shard_map/ppermute | solution.py:629
  (102 other events, 871.3 us)
